TPU v7x, 128 devices: a whole 4x4x4 slice. The times are simulated.
128 devices in a mesh: st: 16 (over y, x), fq: 8 (over z, core).
Axes of the slice: x: 4, y: 4, z: 4, core: 2. Of those that a mesh axis runs over, the one named last changes fastest.
Arguments:
- signals: bfloat16 [1024, 16384], P(('st', 'fq')), may hold values from -6 to 6
- freq_bins: int32 [1024], replicated, may hold values from 1 to 8191, as said below
- sensor_station: int32 [1024], P('st'), may hold values from 0 to 511, as said below
- gain: bfloat16 [1024, 768], P('st'), may hold values from -1.5 to 1.5
- damping: float32 [512, 768], P('st'), may hold values from 0 to 1
- damping_up: float32 [512, 768], P('st'), may hold values from 0 to 1
- phase_speed: float32 [768], replicated, may hold values from 0.5 to 4
Outputs:
- estimate: bfloat16 [512, 768, 1024], P(('st', 'fq'))
Inputs may be any that keep to these rules, and one draw needn't show every extreme that they name: `freq_bins`: distinct bin numbers. `sensor_station`: sensor s sits at one of the 32 stations starting at (s // 64) * 32.
All inputs are finite; a program needn't handle non-finite values.
Results may differ from a plain program's by a relative error of at most 0.015.
Values may be sent and summed in bfloat16 or wider, within the bound.
No kernel may reach another device: no remote copies, remote signals or barrier semaphores. Data moves between devices by JAX's collectives and lax.ppermute only.
A program may use at most 256 MiB of HBM per device.

v0:
```python
import math

import jax
import jax.numpy as jnp
from jax import lax
from jax.sharding import Mesh
from jax.sharding import PartitionSpec as P

NT = 16384
NF = 1024
TOUT = 1024
ST = ("st_0", "st_1")
ST_FQ = ("st_0", "st_1", "fq")


def nothing_yet(array, identity):
    return jax.tree.map(
        lambda a, e: jnp.broadcast_to(jnp.asarray(e, a.dtype), a.shape), array, identity
    )


def prefix_by_axis(array, axes, combine, identity, reverse):
    before = start = nothing_yet(array, identity)
    total = array
    for axis in reversed(axes):
        count, place = (lax.axis_size(axis), lax.axis_index(axis))
        pieces = jax.tree.map(
            lambda part, kind: lax.all_gather(part.astype(kind), axis),
            total,
            (jnp.bfloat16, jnp.bfloat16),
        )
        inside, total = (start, start)
        for k in reversed(range(count)) if reverse else range(count):
            passed = k > place if reverse else k < place
            total = combine(
                total, jax.tree.map(lambda part, own: part[k].astype(own.dtype), pieces, array)
            )
            inside = jax.tree.map(lambda new, old: jnp.where(passed, new, old), total, inside)
        before = combine(inside, before)
    return before


def cmul(left, right):
    return jnp.stack(
        [left[0] * right[0] - left[1] * right[1], left[0] * right[1] + left[1] * right[0]]
    )


def compose(earlier, later):
    return (cmul(later[0], earlier[0]), cmul(later[0], earlier[1]) + later[1])


def phases(steps, freq_bins):
    angle = (steps[:, None] * freq_bins[None, :] % NT).astype(jnp.float32) * (2 * math.pi / NT)
    return (jnp.cos(angle), jnp.sin(angle))


def base_table(count, freq_bins):
    fine = min(count, 128)
    coarse = count // fine
    fine_cos, fine_sin = phases(lax.iota(jnp.int32, fine), freq_bins)
    big_cos, big_sin = phases(lax.iota(jnp.int32, coarse) * fine, freq_bins)
    table_cos = big_cos[:, None, :] * fine_cos[None] - big_sin[:, None, :] * fine_sin[None]
    table_sin = big_sin[:, None, :] * fine_cos[None] + big_cos[:, None, :] * fine_sin[None]
    return (table_cos.reshape(count, -1), table_sin.reshape(count, -1))


def phase_rotated(base_cos, base_sine_table, offset, freq_bins):
    row_cos, row_sin = phases(jnp.reshape(offset, (1,)).astype(jnp.int32), freq_bins)
    return (
        base_cos * row_cos - base_sine_table * row_sin,
        base_sine_table * row_cos + base_cos * row_sin,
    )


def on_device(signals, freq_bins, sensor_station, gain, damping, damping_up, phase_speed):
    sens_dev = signals.shape[0]
    width = min(NT, 2048)
    base_cos, base_sine_table = base_table(width, freq_bins)

    def add_block(index, total):
        start = index * width
        times = start + lax.iota(jnp.int32, width)
        hann = 0.5 - 0.5 * jnp.cos(times.astype(jnp.float32) * (2 * math.pi / NT))
        piece = lax.dynamic_slice_in_dim(signals, start, width, 1)
        windowed = (piece.astype(jnp.float32) * hann[None, :]).astype(jnp.bfloat16)
        turned_cos, shifted_imaginary_factor = phase_rotated(
            base_cos, base_sine_table, start, freq_bins
        )
        table = jnp.concatenate(
            [
                (turned_cos / math.sqrt(NT)).astype(jnp.bfloat16),
                (shifted_imaginary_factor / math.sqrt(NT)).astype(jnp.bfloat16),
            ],
            axis=1,
        )
        return total + jnp.dot(windowed, table, preferred_element_type=jnp.float32)

    spectra = lax.fori_loop(0, NT // width, add_block, jnp.zeros((sens_dev, 2 * NF), jnp.float32))
    spec_re = spectra[:, :NF].astype(jnp.bfloat16)
    spec_im = (-spectra[:, NF:]).astype(jnp.bfloat16)
    spec_re, spec_im = (
        lax.all_to_all(spec_re, "fq", split_axis=1, concat_axis=0, tiled=True),
        lax.all_to_all(spec_im, "fq", split_axis=1, concat_axis=0, tiled=True),
    )
    sens_block = spec_re.shape[0]
    freq_dev = spec_re.shape[1]
    width_state = gain.shape[1]
    st_dev = damping.shape[0]
    own_bins = lax.dynamic_slice_in_dim(freq_bins, lax.axis_index("fq") * freq_dev, freq_dev)
    theta = 2 * math.pi * (own_bins.astype(jnp.float32) / NT)[:, None] * phase_speed[None, :]
    rot_down = jnp.stack([jnp.cos(theta), -jnp.sin(theta)])
    rot_up = jnp.stack([jnp.cos(theta), jnp.sin(theta)])
    local = sensor_station - lax.axis_index(ST) * st_dev
    onehot = (local[None, :] == lax.iota(jnp.int32, st_dev)[:, None]).astype(jnp.bfloat16)
    spec_own = jnp.stack([spec_re, spec_im]).transpose(0, 2, 1)
    selected = onehot[:, None, None, :] * spec_own[None]
    forcing = jnp.dot(selected.reshape(-1, sens_block), gain, preferred_element_type=jnp.float32)
    forcing = forcing.reshape(st_dev, 2, freq_dev, width_state)
    zeros = jnp.zeros((2, freq_dev, width_state), jnp.float32)
    identity = jnp.stack(
        [
            jnp.ones((freq_dev, width_state), jnp.float32),
            jnp.zeros((freq_dev, width_state), jnp.float32),
        ]
    )

    def march_down(carry, inputs):
        state, product = carry
        term, rate = inputs
        factor = rate[None, None, :] * rot_down
        state = cmul(factor, state) + term
        return ((state, cmul(factor, product)), state)

    (last_down, block_down), downstream_fields = lax.scan(
        march_down, (zeros, identity), (forcing, damping)
    )

    def march_upward(carry, inputs):
        state, product = carry
        term, rate, lower = inputs
        factor = rate[None, None, :] * rot_up
        state = cmul(factor, state) + term
        return ((state, cmul(factor, product)), state + lower)

    (first_up, block_up), partial_sum = lax.scan(
        march_upward, (zeros, identity), (forcing, damping_up, downstream_fields), reverse=True
    )
    summary_down, from_below = prefix_by_axis(
        (block_down, last_down), ST, compose, (identity, zeros), False
    )
    summary_up, from_above = prefix_by_axis(
        (block_up, first_up), ST, compose, (identity, zeros), True
    )

    def carry_down(state, rate):
        state = cmul(rate[None, None, :] * rot_down, state)
        return (state, state)

    ending_down, lifted_down = lax.scan(carry_down, from_below, damping)

    def carry_up(state, inputs):
        rate, base, lower = inputs
        state = cmul(rate[None, None, :] * rot_up, state)
        return (state, (base + lower + state).astype(jnp.bfloat16))

    ending_up, state_all = lax.scan(
        carry_up, from_above, (damping_up, partial_sum, lifted_down), reverse=True
    )
    out_cos, out_sin = base_table(TOUT, freq_bins)
    out_cos, out_sin = phase_rotated(out_cos, out_sin, NT - TOUT, freq_bins)
    inverse = jnp.stack(
        [
            (out_cos.T / math.sqrt(NF)).astype(jnp.bfloat16),
            (-out_sin.T / math.sqrt(NF)).astype(jnp.bfloat16),
        ]
    )
    return jnp.einsum(
        "kcfm,cft->kmt",
        lax.all_to_all(state_all, "fq", split_axis=0, concat_axis=2, tiled=True),
        inverse,
        preferred_element_type=jnp.float32,
    ).astype(jnp.bfloat16)


def solution(mesh):
    torus = Mesh(mesh.devices.reshape(4, 4, mesh.shape["fq"]), ("st_0", "st_1", "fq"))
    placed = (P(ST_FQ, None), P(), P(ST), P(ST, None), P(ST, None), P(ST, None), P())
    return jax.shard_map(
        on_device, mesh=torus, in_specs=placed, out_specs=P(ST_FQ, None, None), check_vma=False
    )
```

profile of v0, /device:TPU:1, one launch (start us, length us, event | category | flops | bytes accessed | tf_op | source)
XLA Modules:
  0.0 1048.3 jit_solution(9251666502776828680)
XLA Ops:
  6.5 2.8 fusion.80
  10.4 169.2 %while.84 = (s32[]{:T(128)}, f32[8,2048]{1,0:T(8,128)S(1)}, bf16[8,16384]{1,0:T(8,128)(2,1)}, s32[1024]{0:T(1024)}, f32[128,1024]{1,0:T(8,128)S(1)}, /*index=5*/...) while((s32[]{:T(128)}, f32[8,2048]{1,0:T(8,128)S(1)}, ...), condition=%wide.region_1.2_spmd.clone.clone.clone, body=%wide.region_0.1_spmd.clone.clone.clone.sunk | while | flops 117547008 | bytes 51728600 | solution.py:99
  10.4 7.0 multiply_subtract_fusion.49
  17.5 9.3 fusion.120
  26.9 4.7 fusion.121
  31.6 7.0 multiply_subtract_fusion.49
  38.6 9.3 fusion.120
  48.0 4.7 fusion.121
  52.7 7.0 multiply_subtract_fusion.49
  59.8 9.3 fusion.120
  69.2 4.7 fusion.121
  73.8 7.0 multiply_subtract_fusion.49
  80.9 9.3 fusion.120
  90.3 4.7 fusion.121
  95.0 7.0 multiply_subtract_fusion.49
  102.1 9.3 fusion.120
  111.5 4.7 fusion.121
  116.1 7.0 multiply_subtract_fusion.49
  123.2 9.3 fusion.120
  132.6 4.7 fusion.121
  137.3 7.0 multiply_subtract_fusion.49
  144.4 9.3 fusion.120
  153.8 4.7 fusion.121
  158.4 7.0 multiply_subtract_fusion.49
  165.5 9.3 fusion.120
  174.9 4.7 fusion.121
  180.2 6.8 all-to-all-start.1
  191.7 3.9 all-to-all-start
  195.8 4.5 all-to-all-done
  200.3 10.6 %fusion.42 = f32[32,2,128,768]{3,2,1,0:T(8,128)} fusion(bf16[2,128,64]{1,2,0:T(8,128)(2,1)S(1)} %maximum_bitcast_fusion.2, bf16[32,64]{1,0:T(8,128)(2,1)S(1)} %fusion.96, bf16[64,768]{1,0:T(8,128)(2,1)S(1)} %copy-done), kind=kOutput, calls=%fused_computation.89 | convolution fusion | flops 805830656 | bytes 25300992 | tf_op jit(solution)/shard_map/dot_general | solution.py:118
  211.0 11.4 %broadcast.651.clone.1 = f32[32,2,128,768]{3,2,1,0:T(8,128)} broadcast(f32[]{:T(128)} %constant.262.clone.1), dimensions={} | broadcast | bytes 25165828 | tf_op jit(solution)/shard_map/broadcast.26
  222.4 144.3 %while.82 = (s32[]{:T(128)}, f32[2,128,768]{2,1,0:T(8,128)S(1)}, f32[2,128,768]{2,1,0:T(8,128)S(1)}, f32[32,2,128,768]{3,2,1,0:T(8,128)}, f32[32,768]{1,0:T(8,12...) while((s32[]{:T(128)}, f32[2,128,768]{2,1,0:T(8,128)S(1)}, ...), condition=%wide.region_3.4_spmd.clone, body=%wide.region_2.3_spmd.clone.sunk | while | flops 2555907 | bytes 13378683 | solution.py:135
  369.9 11.8 %broadcast.651.clone = f32[32,2,128,768]{3,2,1,0:T(8,128)} broadcast(f32[]{:T(128)} %constant.262.clone.1), dimensions={} | broadcast | bytes 25165828 | tf_op jit(solution)/shard_map/broadcast.26
  381.7 153.6 %while.83 = (s32[]{:T(128)}, f32[2,128,768]{2,1,0:T(8,128)S(1)}, f32[2,128,768]{2,1,0:T(8,128)S(1)}, f32[32,2,128,768]{3,2,1,0:T(8,128)}, f32[32,768]{1,0:T(8,12...) while((s32[]{:T(128)}, f32[2,128,768]{2,1,0:T(8,128)S(1)}, ...), condition=%wide.region_5.6_spmd.clone, body=%wide.region_4.5_spmd.clone.sunk | while | flops 2752516 | bytes 14165143 | solution.py:146
  384.1 2.4 fusion.117
  403.2 2.5 fusion.117
  408.1 2.4 fusion.117
  432.1 2.5 fusion.117
  470.4 2.5 fusion.117
  484.8 2.5 fusion.117
  489.7 2.4 fusion.117
  494.5 2.5 fusion.117
  518.5 2.4 fusion.117
  537.0 2.8 fusion.60
  551.9 10.3 all-gather.21.cloned.1.call-done
  562.2 2.8 fusion.64
  566.0 24.4 %all-gather.23.cloned.1.call-done = bf16[8,128,768]{2,1,0:T(8,128)(2,1)} async-done(((bf16[2,128,768]{2,1,0:T(8,128)(2,1)}), bf16[8,128,768]{2,1,0:T(8,128)(2,1)}) %all-gather.23.cloned.1.call-update) | async-done | bytes 1572880 | tf_op jit(solution)/shard_map/all_gather | solution.py:28
  602.1 4.8 fusion.46
  607.8 4.2 fusion.49
  613.0 5.5 all-gather.17.cloned.1.call-done
  618.5 2.7 slice_convert_fusion
  621.3 25.4 %all-gather.19.cloned.1.call-done = bf16[4,2,128,768]{3,2,1,0:T(8,128)(2,1)} async-done(((bf16[1,2,128,768]{3,2,1,0:T(8,128)(2,1)}), bf16[4,2,128,768]{3,2,1,0:T(8,128)(2,1)}) %all-gather.19.cloned.1.call-update) | async-done | bytes 1572880 | tf_op jit(solution)/shard_map/all_gather | solution.py:28
  651.7 11.8 %broadcast.651.clone.2 = f32[32,2,128,768]{3,2,1,0:T(8,128)} broadcast(f32[]{:T(128)} %constant.262.clone.1), dimensions={} | broadcast | bytes 25165828 | tf_op jit(solution)/shard_map/broadcast.26
  663.5 62.5 %while.80 = (s32[]{:T(128)}, f32[2,128,768]{2,1,0:T(8,128)S(1)}, f32[32,2,128,768]{3,2,1,0:T(8,128)}, f32[32,768]{1,0:T(8,128)}, f32[2,128,768]{2,1,0:T(8,128)S(1)}, /*index=5*/s32[]{:T(128)}) while((s32[]{:T(128)}, f32[2,128,768]{2,1,0:T(8,128)S(1)}, f32[32,2,128,768]{3,2,1,0:T(8,128)}, f32[32,768]{1,0:T(8,128)}, ...), condition=%wide.region_7.8_spmd, body=%wide.region_6.7_spmd.sunk | while | flops 983042 | bytes 6300757 | solution.py:160
  726.0 2.5 slice_convert_fusion.4
  733.5 6.1 broadcast_in_dim.20
  739.6 103.1 %while.81 = (s32[]{:T(128)}, f32[2,128,768]{2,1,0:T(8,128)S(1)}, bf16[32,2,128,768]{3,2,1,0:T(8,128)(2,1)}, f32[32,768]{1,0:T(8,128)}, f32[2,128,768]{2,1,0:T(8,...) while((s32[]{:T(128)}, f32[2,128,768]{2,1,0:T(8,128)S(1)}, ...), condition=%wide.region_9.10_spmd, body=%wide.region_8.9_spmd.sunk | while | flops 1769475 | bytes 8266873 | solution.py:167
  842.7 6.0 all-to-all-start.2
  849.9 2.5 multiply_add_fusion.7
  852.3 2.8 fusion.41
  855.1 132.4 %all-to-all-done.2 = bf16[32,2,128,768]{3,2,1,0:T(8,128)(2,1)} async-done(((bf16[32,2,128,768]{3,2,1,0:T(8,128)(2,1)}), bf16[32,2,128,768]{3,2,1,0:T(8,128)(2,1)}, u32[]{:S(2)}, u32[]{:S(2)}) %all-to-all-start.2) | async-done | bytes 12582944 | tf_op jit(solution)/shard_map/all_to_all | solution.py:180
  987.6 16.8 %copy.14 = bf16[8,4,2,128,768]{3,0,4,2,1:T(8,128)(2,1)} copy(bf16[8,4,2,128,768]{4,3,2,1,0:T(8,128)(2,1)} %bitcast.78) | data formatting | bytes 25165824 | tf_op jit(solution)/shard_map/all_to_all | solution.py:180
  1004.4 19.3 %all_to_all.46 = bf16[4,2,1024,768]{2,3,1,0:T(8,128)(2,1)} reshape(bf16[4,2,8,128,768]{3,2,4,1,0:T(8,128)(2,1)} %bitcast.534) | data formatting | bytes 25165824 | tf_op jit(solution)/shard_map/all_to_all | solution.py:180
  1023.7 17.7 %bitcast_convert_fusion = bf16[4,768,1024]{2,1,0:T(8,128)(2,1)} fusion(bf16[4,2,1024,768]{2,3,1,0:T(8,128)(2,1)} %all_to_all.46, bf16[1,1024,1024]{2,1,0:T(8,128)(2,1)} %get-tuple-element.811, bf16[1,1024,1024]{2,1,0:T(8,128)(2,1)S(1)} %get-tuple-element.810), kind=kOutput, calls=%fused_computation.70 | convolution fusion | flops 12890144768 | bytes 23068672 | tf_op jit(solution)/shard_map/kcfm,cft->kmt/dot_general | solution.py:178
  (860 shorter events, 487.7 us)
Async XLA Ops:
  6.5 193.8 %copy-start = (bf16[64,768]{1,0:T(8,128)(2,1)S(1)}, bf16[64,768]{1,0:T(8,128)(2,1)}, u32[]{:S(2)}) copy-start(bf16[64,768]{1,0:T(8,128)(2,1)} %param.20) | copy-start | bytes 294916
  10.3 178.1 %copy-start.38 = (f32[768]{0:T(1024)S(1)}, f32[768]{0:T(1024)}, u32[]{:S(2)}) copy-start(f32[768]{0:T(1024)} %param.23) | copy-start | bytes 9220
  10.4 179.5 %copy-start.39 = (s32[64]{0:T(128)S(1)}, s32[64]{0:T(128)}, u32[]{:S(2)}) copy-start(s32[64]{0:T(128)} %param.19) | copy-start | bytes 772
  10.4 7.1 copy-start.35
  31.5 7.0 copy-start.35
  52.7 7.0 copy-start.35
  73.8 7.0 copy-start.35
  95.0 7.0 copy-start.35
  116.1 7.0 copy-start.35
  137.3 7.0 copy-start.35
  158.4 7.0 copy-start.35
  179.6 16.1 %copy-start.3 = (f32[128,1024]{1,0:T(8,128)}, f32[128,1024]{1,0:T(8,128)S(1)}, u32[]{:S(2)}) copy-start(f32[128,1024]{1,0:T(8,128)S(1)} %get-tuple-element.1324) | copy-start | bytes 1572868
  179.6 16.1 %copy-start.5 = (f32[128,1024]{1,0:T(8,128)}, f32[128,1024]{1,0:T(8,128)S(1)}, u32[]{:S(2)}) copy-start(f32[128,1024]{1,0:T(8,128)S(1)} %get-tuple-element.1325) | copy-start | bytes 1572868
  180.2 11.5 %all-to-all-start.1 = ((bf16[8,8,128]{2,0,1:T(8,128)(2,1)}), bf16[8,8,128]{2,0,1:T(8,128)(2,1)S(1)}, u32[]{:S(2)}, u32[]{:S(2)}) async-start(bf16[8,8,128]{2,0,1:T(8,128)(2,1)} %fusion.92), calls=%async_computation.1 | async-start | bytes 32768 | tf_op jit(solution)/shard_map/all_to_all | solution.py:104
  191.7 8.6 all-to-all-start
  195.6 341.4 %all-gather.25.cloned.1.call-start = ((), (), s32[]{:S(2)}) async-start(), calls=%async_computation.9 | async-start | bytes 1966080 | tf_op jit(solution)/shard_map/all_gather | solution.py:28
  200.3 10.6 %copy-start.37 = (f32[2]{0:T(128)S(1)}, f32[2]{0:T(128)}, u32[]{:S(2)}) copy-start(f32[2]{0:T(128)} %constant.263.clone.1) | copy-start | bytes 28
  366.8 1.0 copy-start.2
  367.6 173.2 %all-gather.27.cloned.1.call-start = ((), (), s32[]{:S(2)}) async-start(), calls=%async_computation.10 | async-start | bytes 1966080 | tf_op jit(solution)/shard_map/all_gather | solution.py:28
  369.7 192.5 %all-gather.21.cloned.1.call-start = ((), (), s32[]{:S(2)}) async-start(), calls=%async_computation.7 | async-start | bytes 1966080 | tf_op jit(solution)/shard_map/all_gather | solution.py:28
  536.1 54.3 %all-gather.23.cloned.1.call-start = ((), (), s32[]{:S(2)}) async-start(), calls=%async_computation.8 | async-start | bytes 1966080 | tf_op jit(solution)/shard_map/all_gather | solution.py:28
  537.0 81.6 %all-gather.17.cloned.1.call-start = ((), (), s32[]{:S(2)}) async-start(), calls=%async_computation.5 | async-start | bytes 1966080 | tf_op jit(solution)/shard_map/all_gather | solution.py:28
  540.8 4.5 copy-start.7
  540.8 4.5 copy-start.26
  543.5 0.8 copy-start.14
  543.5 1.8 copy-start.15
  546.7 2.3 copy-start.18
  546.7 2.3 copy-start.19
  546.7 2.3 copy-start.22
  546.7 2.3 copy-start.23
  549.0 2.9 copy-start.12
  549.0 2.9 copy-start.13
  550.0 96.7 %all-gather.19.cloned.1.call-start = ((), (), s32[]{:S(2)}) async-start(), calls=%async_computation.6 | async-start | bytes 1966080 | tf_op jit(solution)/shard_map/all_gather | solution.py:28
  551.9 174.1 %all-gather.13.cloned.1.call-start = ((), (), s32[]{:S(2)}) async-start(), calls=%async_computation.3 | async-start | bytes 1966080 | tf_op jit(solution)/shard_map/all_gather | solution.py:28
  590.4 4.5 copy-start.8
  590.4 4.5 copy-start.27
  593.0 0.7 copy-start.16
  593.0 1.8 copy-start.17
  596.2 2.6 copy-start.20
  596.2 2.6 copy-start.21
  596.2 2.6 copy-start.24
  596.2 2.6 copy-start.25
  599.6 128.9 %all-gather.15.cloned.1.call-start = ((), (), s32[]{:S(2)}) async-start(), calls=%async_computation.4 | async-start | bytes 1966080 | tf_op jit(solution)/shard_map/all_gather | solution.py:28
  599.9 7.9 copy-start.9
  646.7 3.5 copy-start.28
  646.7 3.7 copy-start.10
  650.2 1.1 copy-start.30
  650.3 1.2 copy-start.33
  650.3 1.2 copy-start.34
  728.5 3.6 copy-start.11
  732.0 1.1 copy-start.29
  732.1 1.2 copy-start.31
  732.1 1.3 copy-start.32
  842.7 6.0 copy-start.6
  842.7 6.2 copy-start.4
  842.7 6.4 copy-start.36
  842.7 144.8 %all-to-all-start.2 = ((bf16[32,2,128,768]{3,2,1,0:T(8,128)(2,1)}), bf16[32,2,128,768]{3,2,1,0:T(8,128)(2,1)}, u32[]{:S(2)}, u32[]{:S(2)}) async-start(bf16[32,2,128,768]{3,2,1,0:T(8,128)(2,1)} %get-tuple-element.537), calls=%async_computation.2 | async-start | bytes 25165824 | tf_op jit(solution)/shard_map/all_to_all | solution.py:180
  1023.7 17.7 %copy-start.1 = (bf16[64,768]{1,0:T(8,128)(2,1)S(1)}, bf16[64,768]{1,0:T(8,128)(2,1)}, u32[]{:S(2)}) copy-start(bf16[64,768]{1,0:T(8,128)(2,1)} %param.20) | copy-start | bytes 294916
Sparse Core Ops, SparseCore 0:
  367.8 26.0 all-gather.24
  395.5 26.5 all-gather.26
  536.2 25.9 all-gather.20
  563.8 26.5 all-gather.22
  591.9 26.6 all-gather.16
  620.1 26.5 all-gather.18
  648.3 26.5 all-gather.12
  676.6 26.5 all-gather.14
where the time goes:
time: 1060 us; the launch traced here: 1050 us
  other arithmetic  565 us (53%)
  waiting for transfers between devices  204 us (19%)
  local copies, waits for them, and re-layouts  178 us (17%)
  matrix products  65.7 us (6%)
  starting transfers between devices  17.3 us (2%)
  between operations  14.1 us (1%)
    dynamic_update_slice x96, other arithmetic, on_device(): lax.scan(march_down, (zeros, identity), (forcing, damping))  179 us
    all_to_all x1, waiting for transfers between devices, on_device(): lax.all_to_all(state_all, 'fq', split_axis=0, concat_axis=2, tiled=True)  132 us
    dynamic_slice x128, local copies, waits for them, and re-layouts, on_device(): lax.scan(march_down, (zeros, identity), (forcing, damping))  96.3 us
    convert_element_type x8, other arithmetic, add_block(): (turned_cos / math.sqrt(NT)).astype(jnp.bfloat16)  74.6 us
    dynamic_update_slice x32, other arithmetic, on_device(): lax.scan(carry_up, from_above, (damping_up, partial_sum, lifted_down), re...  71.7 us
    all_gather x8, waiting for transfers between devices, prefix_by_axis(): lax.all_gather(part.astype(kind), axis)  65.6 us
    sub x8, other arithmetic, base_table(): big_cos[:, None, :] * fine_cos[None] - big_sin[:, None, :] * fine_sin[None]  56.2 us
    add x32, other arithmetic, march_upward(): state = cmul(factor, state) + term  39.8 us
  transfers between devices with their start and end apart: 11, of which 7 were waited for; matrix products, arithmetic and copies ran while one was open for 29% of the time, Pallas kernels for 0%

commit v1 on v0

v1 whole, which is shorter than its diff:
```python
import math

import jax
import jax.numpy as jnp
from jax import lax
from jax.experimental import pallas as pl
from jax.experimental.pallas import tpu as pltpu
from jax.sharding import Mesh
from jax.sharding import PartitionSpec as P

NT = 16384
TOUT = 1024
BLOCK = 32
GROUP = 8
OWN = 4
TILE = 128
SLICE = 48
ALL = ("st", "z", "core")
FQ = ("z", "core")
MIB = 1 << 20

COS = (1.0, -19.739208221435547, 64.93939208984375, -85.45665740966797, 60.242130279541016,
       -26.4046688079834, 7.800131797790527, -1.4531123638153076)
SIN = (6.2831854820251465, -41.34170150756836, 81.60513305664062, -76.70301818847656,
       42.02592849731445, -14.899847984313965, 3.238137722015381)


def horner(terms, y):
    total = y * terms[-1] + terms[-2]
    for term in terms[-3::-1]:
        total = total * y + term
    return total


def cos_sin(turns):
    r = turns - jnp.floor(turns + 0.5)
    y = r * r
    return horner(COS, y), r * horner(SIN, y)


def table_turns(steps, bins):
    return ((steps * bins) & (NT - 1)).astype(jnp.float32) * (1.0 / NT)


def spectrum_kernel(signals_ref, bins_ref, out_ref, windowed):
    sensors = out_ref.shape[1]
    coarse = lax.broadcasted_iota(jnp.int32, (128, 128), 0)
    fine = lax.broadcasted_iota(jnp.int32, (128, 128), 1)

    @pl.when(pl.program_id(0) == 0)
    def _():
        times = (coarse * 128 + fine).astype(jnp.float32)
        hann = 0.5 - 0.5 * cos_sin(times * (1.0 / NT))[0]
        for s in range(sensors):
            rows = pl.ds(s * 128, 128)
            windowed[rows, :] = (signals_ref[rows, :].astype(jnp.float32) * hann).astype(jnp.bfloat16)

    bins = bins_ref[0, 0:1, :]
    c1, s1 = cos_sin(table_turns(coarse, bins))
    table = jnp.concatenate(
        [(c1 * (1 / 128)).astype(jnp.bfloat16), (s1 * (-1 / 128)).astype(jnp.bfloat16)], axis=1
    )
    c2, s2 = cos_sin(table_turns(coarse * 128, bins))
    for s in range(sensors):
        part = jnp.dot(windowed[pl.ds(s * 128, 128), :], table, preferred_element_type=jnp.float32)
        re, im = part[:, :TILE], part[:, TILE:]
        out_ref[0, s:s + 1, :TILE] = jnp.sum(re * c2 + im * s2, axis=0, keepdims=True)
        out_ref[0, s:s + 1, TILE:] = jnp.sum(im * c2 - re * s2, axis=0, keepdims=True)


def spectrum(signals, freq_bins):
    sensors = signals.shape[0]
    tiles = freq_bins.shape[0] // TILE
    bins = jnp.broadcast_to(freq_bins.reshape(tiles, 1, TILE), (tiles, 8, TILE))
    return pl.pallas_call(
        spectrum_kernel,
        grid=(tiles,),
        in_specs=[
            pl.BlockSpec((sensors * 128, 128), lambda q: (0, 0)),
            pl.BlockSpec((1, 8, TILE), lambda q: (q, 0, 0)),
        ],
        out_specs=pl.BlockSpec((1, sensors, 2 * TILE), lambda q: (q, 0, 0)),
        out_shape=jax.ShapeDtypeStruct((tiles, sensors, 2 * TILE), jnp.float32),
        scratch_shapes=[pltpu.VMEM((sensors * 128, 128), jnp.bfloat16)],
        compiler_params=pltpu.CompilerParams(vmem_limit_bytes=24 * MIB),
        cost_estimate=pl.CostEstimate(flops=2 * 10**9, bytes_accessed=10**6, transcendentals=0),
        name="spectrum",
    )(signals.reshape(sensors * 128, 128), bins)


def inverse_kernel(bins_ref, out_ref):
    times = lax.broadcasted_iota(jnp.int32, (TILE, TOUT), 1) + (NT - TOUT)
    c, s = cos_sin(table_turns(times, bins_ref[:, 0:1]))
    out_ref[:TILE, :] = (c * (1 / 32)).astype(jnp.bfloat16)
    out_ref[TILE:, :] = (s * (-1 / 32)).astype(jnp.bfloat16)


def inverse_table(freq_bins):
    tiles = freq_bins.shape[0] // TILE
    bins = jnp.broadcast_to(freq_bins[:, None], (tiles * TILE, 128))
    return pl.pallas_call(
        inverse_kernel,
        grid=(tiles,),
        in_specs=[pl.BlockSpec((TILE, 128), lambda q: (q, 0))],
        out_specs=pl.BlockSpec((2 * TILE, TOUT), lambda q: (q, 0)),
        out_shape=jax.ShapeDtypeStruct((tiles * 2 * TILE, TOUT), jnp.bfloat16),
        compiler_params=pltpu.CompilerParams(vmem_limit_bytes=24 * MIB),
        cost_estimate=pl.CostEstimate(flops=4 * 10**9, bytes_accessed=5 * 10**6, transcendentals=0),
        name="inverse_table",
    )(bins)


def step(rate, c, s, re, im, f_re, f_im):
    return rate * (c * re - s * im) + f_re, rate * (c * im + s * re) + f_im


def march_kernel(tables_ref, spec_ref, rot_ref, out_ref, sel, force):
    blocks = tables_ref.shape[0]

    def forcing(block, slot):
        gain = tables_ref[block, :SLICE, :64]
        local = tables_ref[block, SLICE:SLICE + 1, :64]
        for k in range(BLOCK):
            sel[slot, pl.ds(k * SLICE, SLICE), :] = jnp.where(
                local == jnp.float32(k), gain, 0.0
            ).astype(jnp.bfloat16)
        force[slot] = jnp.dot(sel[slot], spec_ref[block], preferred_element_type=jnp.float32)

    def body(b, carry):
        d_re, d_im, u_re, u_im = carry
        up = blocks - 1 - b
        forcing(b, 0)
        forcing(up, 1)
        c, s = rot_ref[0], rot_ref[1]
        down_rates = tables_ref[b, :SLICE, :]
        up_rates = tables_ref[up, :SLICE, :]
        for k in range(BLOCK):
            if k % GROUP == 0:
                group = 2 * (b * (BLOCK // GROUP) + k // GROUP)
                out_ref[group, :SLICE, :] = d_re.astype(jnp.bfloat16)
                out_ref[group, SLICE:, :] = d_im.astype(jnp.bfloat16)
            rows = pl.ds(k * SLICE, SLICE)
            d_re, d_im = step(
                down_rates[:, 64 + k:65 + k], c, -s, d_re, d_im,
                force[0, rows, :TILE], force[0, rows, TILE:],
            )
            j = BLOCK - 1 - k
            if j % GROUP == GROUP - 1:
                group = 2 * (up * (BLOCK // GROUP) + j // GROUP) + 1
                out_ref[group, :SLICE, :] = u_re.astype(jnp.bfloat16)
                out_ref[group, SLICE:, :] = u_im.astype(jnp.bfloat16)
            rows = pl.ds(j * SLICE, SLICE)
            u_re, u_im = step(
                up_rates[:, 96 + j:97 + j], c, s, u_re, u_im,
                force[1, rows, :TILE], force[1, rows, TILE:],
            )
        return d_re, d_im, u_re, u_im

    zero = jnp.zeros((SLICE, TILE), jnp.float32)
    lax.fori_loop(0, blocks, body, (zero, zero, zero, zero))


def entering_states(tables, spec, rot):
    blocks = tables.shape[0]
    return pl.pallas_call(
        march_kernel,
        out_shape=jax.ShapeDtypeStruct(
            (2 * blocks * BLOCK // GROUP, 2 * SLICE, TILE), jnp.bfloat16
        ),
        in_specs=[pl.BlockSpec(memory_space=pltpu.VMEM)] * 3,
        out_specs=pl.BlockSpec(memory_space=pltpu.VMEM),
        scratch_shapes=[
            pltpu.VMEM((2, BLOCK * SLICE, 64), jnp.bfloat16),
            pltpu.VMEM((2, BLOCK * SLICE, 2 * TILE), jnp.float32),
        ],
        compiler_params=pltpu.CompilerParams(vmem_limit_bytes=24 * MIB),
        cost_estimate=pl.CostEstimate(flops=20 * 10**9, bytes_accessed=5 * 10**6, transcendentals=0),
        name="entering_states",
    )(tables, spec, rot)


def estimate_kernel(
    core_ref, near_ref, far_ref, gain_ref, rates_ref, spec_ref, omega_ref, inverse_ref,
    out_ref, state, force, kept,
):
    slices = near_ref.shape[0]
    tiles = near_ref.shape[1]
    core = core_ref[0]

    def fill(q, unused):
        lane = pl.multiple_of(q * 2 * TILE, 2 * TILE)
        omega = omega_ref[q, 0:1, :]
        for t in range(slices):
            force[...] = jnp.dot(gain_ref[t], spec_ref[q], preferred_element_type=jnp.float32)
            rates = rates_ref[t]
            c, s = cos_sin(omega * rates[:, GROUP + OWN:GROUP + OWN + 1])
            re = near_ref[t, q, :SLICE, :].astype(jnp.float32)
            im = near_ref[t, q, SLICE:, :].astype(jnp.float32)
            for i in range(OWN):
                rows = pl.ds((GROUP - 1 - i) * SLICE, SLICE)
                re, im = step(
                    rates[:, GROUP + i:GROUP + i + 1], c, -s, re, im,
                    force[rows, :TILE], force[rows, TILE:],
                )
                kept[i, 0], kept[i, 1] = re, im
            re = far_ref[t, q, :SLICE, :].astype(jnp.float32)
            im = far_ref[t, q, SLICE:, :].astype(jnp.float32)
            for i in range(GROUP):
                rows = pl.ds(i * SLICE, SLICE)
                re, im = step(
                    rates[:, i:i + 1], c, s, re, im, force[rows, :TILE], force[rows, TILE:]
                )
                if i >= GROUP - OWN:
                    n = GROUP - 1 - i
                    own = jnp.where(core == 0, n, OWN - 1 - n)
                    rows = pl.ds(t * SLICE, SLICE)
                    state[own, rows, pl.ds(lane, TILE)] = (re + kept[n, 0]).astype(jnp.bfloat16)
                    state[own, rows, pl.ds(lane + TILE, TILE)] = (im + kept[n, 1]).astype(jnp.bfloat16)
        return unused

    lax.fori_loop(0, tiles, fill, 0)
    height = slices * SLICE

    def multiply(n, unused):
        columns = pl.ds(pl.multiple_of(n * 256, 256), 256)
        out = jnp.dot(
            state[...].reshape(OWN * height, 2 * tiles * TILE), inverse_ref[:, columns],
            preferred_element_type=jnp.float32,
        )
        out_ref[:, :, columns] = out.astype(jnp.bfloat16).reshape(OWN, height, 256)
        return unused

    lax.fori_loop(0, TOUT // 256, multiply, 0)


def estimates(core, near, far, gain, rates, spec, omega, inverse):
    slices, tiles = near.shape[:2]
    per = 4
    once = pl.Buffered(1)
    whole = lambda a: pl.BlockSpec(a.shape, lambda i: (0,) * a.ndim, pipeline_mode=once)
    return pl.pallas_call(
        estimate_kernel,
        grid=(slices // per,),
        in_specs=[
            pl.BlockSpec(memory_space=pltpu.SMEM),
            pl.BlockSpec((per, tiles, 2 * SLICE, TILE), lambda i: (i, 0, 0, 0)),
            pl.BlockSpec((per, tiles, 2 * SLICE, TILE), lambda i: (i, 0, 0, 0)),
            pl.BlockSpec((per, GROUP * SLICE, 64), lambda i: (i, 0, 0)),
            pl.BlockSpec((per, SLICE, 128), lambda i: (i, 0, 0)),
            whole(spec),
            whole(omega),
            whole(inverse),
        ],
        out_specs=pl.BlockSpec((OWN, per * SLICE, TOUT), lambda i: (0, i, 0)),
        out_shape=jax.ShapeDtypeStruct((OWN, slices * SLICE, TOUT), jnp.bfloat16),
        scratch_shapes=[
            pltpu.VMEM((OWN, per * SLICE, 2 * tiles * TILE), jnp.bfloat16),
            pltpu.VMEM((GROUP * SLICE, 2 * TILE), jnp.float32),
            pltpu.VMEM((OWN, 2, SLICE, TILE), jnp.float32),
        ],
        compiler_params=pltpu.CompilerParams(vmem_limit_bytes=40 * MIB),
        cost_estimate=pl.CostEstimate(flops=40 * 10**9, bytes_accessed=20 * 10**6, transcendentals=0),
        name="estimates",
    )(core, near, far, gain, rates, spec, omega, inverse)


def on_device(signals, freq_bins, sensor_station, gain, damping, damping_up, phase_speed):
    st, z, core = (lax.axis_index(axis) for axis in ALL)
    blocks = lax.axis_size("st")
    tiles = freq_bins.shape[0] // TILE
    sensors = sensor_station.shape[0]
    local = sensor_station - st * BLOCK
    wide_gain = gain.astype(jnp.float32)

    columns = jnp.concatenate([wide_gain, damping, damping_up], axis=0)
    columns = columns.T.reshape(blocks, SLICE, sensors + 2 * BLOCK)
    places = jnp.pad(local.astype(jnp.float32), (0, 2 * BLOCK))
    places = jnp.broadcast_to(places, (blocks, 8, sensors + 2 * BLOCK))
    tables = lax.all_to_all(
        jnp.concatenate([columns, places], axis=1), "st", split_axis=0, concat_axis=0, tiled=True
    )

    spec = spectrum(signals, freq_bins).astype(jnp.bfloat16)
    to_all = jnp.broadcast_to(spec[None], (blocks,) + spec.shape).reshape((-1,) + spec.shape[1:])
    spec_tile = lax.all_to_all(to_all, ALL, split_axis=0, concat_axis=0, tiled=True)
    spec_tile = spec_tile.reshape(blocks, sensors, 2 * TILE)
    to_fq = jnp.broadcast_to(spec[None], (tiles,) + spec.shape)
    spec_block = lax.all_to_all(to_fq, FQ, split_axis=0, concat_axis=0, tiled=True)
    spec_block = spec_block.transpose(1, 0, 2, 3).reshape(tiles, sensors, 2 * TILE)

    omega = (freq_bins.astype(jnp.float32) / NT).reshape(tiles, 1, TILE)
    own_omega = lax.dynamic_index_in_dim(omega, z * 2 + core, 0, keepdims=False)
    own_speed = lax.dynamic_slice_in_dim(phase_speed, st * SLICE, SLICE)
    theta = 2 * math.pi * own_omega * own_speed[:, None]
    rot = jnp.stack([jnp.cos(theta), jnp.sin(theta)])
    entering = entering_states(tables, spec_tile, rot)

    near = lax.all_to_all(entering, ALL, split_axis=0, concat_axis=0, tiled=True)
    far = lax.ppermute(near, "core", [(0, 1), (1, 0)])
    shape = (blocks, tiles, 2 * SLICE, TILE)

    first = z * GROUP
    eight = lax.iota(jnp.int32, GROUP)
    far_order = first + jnp.where(core == 0, GROUP - 1 - eight, eight)
    near_order = far_order[:GROUP - OWN - 1:-1]
    far_rates = jnp.where(core == 0, damping_up[far_order], damping[far_order])
    near_rates = jnp.where(core == 0, damping[near_order], damping_up[near_order])
    turn = jnp.where(core == 0, phase_speed, -phase_speed)[None]
    rates = jnp.concatenate([far_rates, near_rates, turn], axis=0)
    rates = jnp.pad(rates, ((0, 128 - rates.shape[0]), (0, 0))).T.reshape(blocks, SLICE, 128)
    slices_gain = gain.T.reshape(blocks, 1, SLICE, sensors)
    at = (local[None, :] == far_order[:, None])[None, :, None, :]
    own_gain = jnp.where(at, slices_gain, 0).reshape(blocks, GROUP * SLICE, sensors)

    return estimates(
        core.reshape(1).astype(jnp.int32),
        near.reshape(shape),
        far.reshape(shape),
        own_gain,
        rates,
        spec_block,
        jnp.broadcast_to(omega, (tiles, 8, TILE)),
        inverse_table(freq_bins),
    )


def solution(mesh):
    torus = Mesh(mesh.devices.reshape(mesh.shape["st"], 4, 2), ALL)
    placed = (P(ALL, None), P(), P("st"), P("st", None), P("st", None), P("st", None), P())
    return jax.shard_map(
        on_device, mesh=torus, in_specs=placed, out_specs=P(ALL, None, None), check_vma=False
    )
```

time: 1060 us -> 177 us (0.17); the launches traced: 1050 us -> 176 us
  other arithmetic: 565 us -> 6.67 us
  waiting for transfers between devices: 204 us -> 19.4 us
  local copies, waits for them, and re-layouts: 178 us -> 13.2 us
  Pallas kernels: 0 us -> 70.2 us
  matrix products: 65.7 us -> 0 us
  blocking collectives: 0 us -> 45.8 us
  between operations: 14.1 us -> 0.32 us
    dynamic_update_slice x128 -> x0, other arithmetic: 251 us -> none  [the longest x96 179 us: on_device(): lax.scan(march_down, (zeros, identity), (forcing, damping))]
    all_to_all x3, waiting for transfers between devices: 139 us -> 19.4 us  [the longest x1 13.3 us: on_device(): lax.all_to_all(to_all, ALL, split_axis=0, concat_axis=0, tiled=True)]
    dynamic_slice x128 -> x1, local copies, waits for them, and re-layouts: 96.3 us -> 0.08 us  [on_device(): own_speed = lax.dynamic_slice_in_dim(phase_speed, st * SLICE, SLICE)]
    add x79 -> x1, other arithmetic: 94.6 us -> 0.01 us  [on_device(): far_order = first + jnp.where(core == 0, GROUP - 1 - eight, eight)]
    convert_element_type x19 -> x3, other arithmetic: 93.8 us -> 1.62 us  [the longest x1 0.95 us: on_device(): wide_gain = gain.astype(jnp.float32)]
    sub x165 -> x0, other arithmetic: 88 us -> none  [the longest x8 56.2 us: base_table(): big_cos[:, None, :] * fine_cos[None] - big_sin[:, None, :] * fine_sin[None]]
    pallas_call x0 -> x4, Pallas kernels: none -> 70.2 us  [the longest x1 43.4 us: estimates(): pl.pallas_call(estimate_kernel, grid=(slices // per,), in_specs=[pl.Block...]
    dot_general x10 -> x0, matrix products: 65.7 us -> none  [the longest x8 37.4 us: add_block(): return total + jnp.dot(windowed, table, preferred_element_type=jnp.float32)]
  transfers between devices with their start and end apart: 11 -> 4, of which waited for: 7 -> 2; matrix products, arithmetic and copies ran while one was open for 29% -> 6% of each run, Pallas kernels for 0% -> 7%
where the time goes in v1:
time: 177 us; the launch traced here: 176 us
  Pallas kernels  70.2 us (40%)
  blocking collectives  45.8 us (26%)
  starting transfers between devices  20.9 us (12%)
  waiting for transfers between devices  19.4 us (11%)
  local copies, waits for them, and re-layouts  13.2 us (7%)
  other arithmetic  6.67 us (4%)
    all_to_all x1, blocking collectives, on_device(): lax.all_to_all(entering, ALL, split_axis=0, concat_axis=0, tiled=True)  45.8 us
    pallas_call x1, Pallas kernels, estimates(): pl.pallas_call(estimate_kernel, grid=(slices // per,), in_specs=[pl.Block...  43.4 us
    pallas_call x1, Pallas kernels, entering_states(): pl.pallas_call(march_kernel, out_shape=jax.ShapeDtypeStruct((2 * blocks *...  13.9 us
    all_to_all x1, waiting for transfers between devices, on_device(): lax.all_to_all(to_all, ALL, split_axis=0, concat_axis=0, tiled=True)  13.3 us
    pallas_call x1, Pallas kernels, inverse_table(): pl.pallas_call(inverse_kernel, grid=(tiles,), in_specs=[pl.BlockSpec((TIL...  9.35 us
    all_to_all x1, starting transfers between devices, on_device(): lax.all_to_all(to_all, ALL, split_axis=0, concat_axis=0, tiled=True)  7.97 us
    all_to_all x1, starting transfers between devices, on_device(): lax.all_to_all(jnp.concatenate([columns, places], axis=1), 'st', split_ax...  7.58 us
    all_to_all x1, waiting for transfers between devices, on_device(): lax.all_to_all(jnp.concatenate([columns, places], axis=1), 'st', split_ax...  6.1 us
  transfers between devices with their start and end apart: 4, of which 2 were waited for; matrix products, arithmetic and copies ran while one was open for 6% of the time, Pallas kernels for 7%

profile of v1, /device:TPU:1, one launch (start us, length us, event | category | flops | bytes accessed | tf_op | source)
XLA Modules:
  0.0 176.4 jit_solution(5695943049295102415)
XLA Ops:
  0.0 0.0 copy-start.6
  0.0 0.0 copy-start.7
  0.0 0.9 convert_element_type.18
  1.0 1.0 maximum_bitcast_fusion
  1.9 0.2 copy.14
  2.1 0.7 fusion.5
  2.8 0.8 pad_maximum_fusion
  3.6 7.6 %all-to-all-start = ((f32[16,56,128]{2,1,0:T(8,128)}), f32[16,56,128]{2,1,0:T(8,128)S(1)}, u32[]{:S(2)}, u32[]{:S(2)}) async-start(f32[16,56,128]{2,1,0:T(8,128)} %pad_maximum_fusion), calls=%async_computation | async-start | bytes 917504 | tf_op jit(solution)/shard_map/all_to_all | solution.py:279
  11.2 0.0 copy-done.6
  11.2 0.1 reshape.189.signals_ref
  11.3 0.0 copy-done.7
  11.3 0.0 copy-start.8
  11.3 3.6 %spectrum.1 = f32[8,8,256]{2,1,0:T(8,128)S(1)} custom-call(bf16[1024,128]{1,0:T(8,128)(2,1)S(1)} %reshape.189.signals_ref, s32[8,8,128]{2,1,0:T(8,128)S(1)} %broadcast_in_dim.78.bins_ref), custom_call_target="tpu_custom_call" | custom-call | flops 2000000000 | bytes 1000000 | tf_op jit(solution)/shard_map/spectrum/pallas_call | solution.py:75
  14.9 6.1 %all-to-all-done.tables_ref = f32[16,56,128]{2,1,0:T(8,128)S(1)} async-done(((f32[16,56,128]{2,1,0:T(8,128)}), f32[16,56,128]{2,1,0:T(8,128)S(1)}, u32[]{:S(2)}, u32[]{:S(2)}) %all-to-all-start) | async-done | bytes 458784 | tf_op jit(solution)/shard_map/all_to_all | solution.py:279
  21.0 0.8 broadcast_in_dim.79
  21.9 8.0 %all-to-all-start.1 = ((bf16[128,8,256]{2,1,0:T(8,128)(2,1)}), bf16[128,8,256]{2,1,0:T(8,128)(2,1)S(1)}, u32[]{:S(2)}, u32[]{:S(2)}) async-start(bf16[128,8,256]{2,1,0:T(8,128)(2,1)} %bitcast.4), calls=%async_computation.1 | async-start | bytes 1048576 | tf_op jit(solution)/shard_map/all_to_all | solution.py:285
  29.9 0.0 copy-done.8
  29.9 0.1 dynamic_slice.8
  30.0 0.2 multiply_cosine_fusion
  30.2 13.3 %all-to-all-done.1 = bf16[128,8,256]{2,1,0:T(8,128)(2,1)S(1)} async-done(((bf16[128,8,256]{2,1,0:T(8,128)(2,1)}), bf16[128,8,256]{2,1,0:T(8,128)(2,1)S(1)}, u32[]{:S(2)}, u32[]{:S(2)}) %all-to-all-start.1) | async-done | bytes 524320 | tf_op jit(solution)/shard_map/all_to_all | solution.py:285
  43.4 13.9 %entering_states.1 = bf16[128,96,128]{2,1,0:T(8,128)(2,1)S(1)} custom-call(f32[16,56,128]{2,1,0:T(8,128)S(1)} %all-to-all-done.tables_ref, bf16[16,64,256]{2,1,0:T(8,128)(2,1)S(1)} %bitcast.30, f32[2,48,128]{2,1,0:T(8,128)S(1)} %pad_maximum_fusion.1.rot_ref), custom_call_target="tpu_custom_call" | custom-call | flops 20000000000 | bytes 5000000 | tf_op jit(solution)/shard_map/entering_states/pallas_call | solution.py:165
  57.3 0.0 copy-start.4
  57.3 0.0 copy-start.3
  57.3 0.0 copy-start.5
  57.3 45.8 %all_to_all.20 = bf16[128,96,128]{2,1,0:T(8,128)(2,1)S(1)} all-to-all(bf16[128,96,128]{2,1,0:T(8,128)(2,1)S(1)} %entering_states.1), channel_id=1, replica_groups=mesh['st'=16,'z'=4,'core'=2] {'st','z','core'}, dimensions={0} | all-to-all | bytes 6291456 | tf_op jit(solution)/shard_map/all_to_all | solution.py:298
  103.1 1.3 collective-permute-start
  104.4 0.7 broadcast_in_dim.89
  105.2 4.0 %all-to-all-start.3 = ((bf16[8,8,8,256]{3,2,1,0:T(8,128)(2,1)}), bf16[8,8,8,256]{3,2,1,0:T(8,128)(2,1)}, u32[]{:S(2)}, u32[]{:S(2)}) async-start(bf16[8,8,8,256]{3,2,1,0:T(8,128)(2,1)} %broadcast_in_dim.89), calls=%async_computation.3 | async-start | bytes 524288 | tf_op jit(solution)/shard_map/all_to_all | solution.py:288
  109.2 0.1 slice.3
  109.3 0.1 rev.3
  109.4 0.0 copy-done.4
  109.4 0.6 gather_fusion.3
  109.9 0.0 copy-done.3
  110.0 0.6 gather_fusion.2
  110.6 0.6 gather_fusion.1
  111.1 0.6 gather_fusion
  111.7 0.0 copy-done.5
  111.7 0.8 copy.18
  112.6 0.8 fusion
  113.4 1.1 copy.16
  114.5 0.1 broadcast_compare_fusion
  114.6 2.2 %bitcast_select_fusion.gain_ref = bf16[16,384,64]{2,1,0:T(8,128)(2,1)} fusion(pred[384,64]{1,0:T(8,128)(4,1)S(1)} %bitcast.35, bf16[16,48,64]{2,1,0:T(8,128)(2,1)} %bitcast.33), kind=kLoop, calls=%fused_computation.4 | loop fusion | flops 393216 | bytes 909312 | tf_op jit(solution)/shard_map/jit(_where)/select_n | solution.py:313
  116.8 0.2 broadcast_in_dim.92.bins_ref
  117.0 9.4 %inverse_table.1.inverse_ref = bf16[2048,1024]{1,0:T(8,128)(2,1)S(1)} custom-call(s32[1024,128]{1,0:T(8,128)S(1)} %broadcast_in_dim.92.bins_ref), custom_call_target="tpu_custom_call" | custom-call | flops 4000000000 | bytes 5000000 | tf_op jit(solution)/shard_map/inverse_table/pallas_call | solution.py:101
  126.4 0.0 copy-start.1
  126.4 2.0 %copy-done.1 = bf16[2048,1024]{1,0:T(8,128)(2,1)} copy-done((bf16[2048,1024]{1,0:T(8,128)(2,1)}, bf16[2048,1024]{1,0:T(8,128)(2,1)S(1)}, u32[]{:S(2)}) %copy-start.1) | copy-done | bytes 4194328
  128.4 0.0 all-to-all-done.3
  128.4 1.0 copy_bitcast_fusion.spec_ref
  129.4 0.0 collective-permute-done
  129.4 0.0 copy-start
  129.4 1.4 copy-done
  130.8 0.0 copy-start.2
  130.8 2.2 %copy-done.2 = bf16[2048,1024]{1,0:T(8,128)(2,1)S(1)} copy-done((bf16[2048,1024]{1,0:T(8,128)(2,1)S(1)}, bf16[2048,1024]{1,0:T(8,128)(2,1)}, u32[]{:S(2)}) %copy-start.2) | copy-done | bytes 4194328
  133.0 43.4 %estimates.1 = bf16[4,768,1024]{2,1,0:T(8,128)(2,1)} custom-call(s32[1]{0:T(128)} %bitcast.core_ref, bf16[16,8,96,128]{3,2,1,0:T(8,128)(2,1)S(1)} %bitcast.29, bf16[16,8,96,128]{3,2,1,0:T(8,128)(2,1)} %bitcast.9.far_ref, bf16[16,384,64]{2,1,0:T(8,128)(2,1)S(1)} %copy-done, f32[16,48,128]{2,1,0:T(8,128)S(1)} %bitcast.31, ...), custom_call_target="tpu_custom_call" | custom-call | flops 40000000000 | bytes 20000000 | tf_op jit(solution)/shard_map/estimates/pallas_call | solution.py:241
  (18 shorter events, 0.1 us)
Async XLA Ops:
  0.0 11.2 %copy-start.6 = (bf16[8,16384]{1,0:T(8,128)(2,1)S(1)}, bf16[8,16384]{1,0:T(8,128)(2,1)}, u32[]{:S(2)}) copy-start(bf16[8,16384]{1,0:T(8,128)(2,1)} %param.7) | copy-start | bytes 786436
  0.0 11.3 %copy-start.7 = (s32[1024]{0:T(1024)S(1)}, s32[1024]{0:T(1024)}, u32[]{:S(2)}) copy-start(s32[1024]{0:T(1024)} %param.8) | copy-start | bytes 12292
  3.6 17.5 %all-to-all-start = ((f32[16,56,128]{2,1,0:T(8,128)}), f32[16,56,128]{2,1,0:T(8,128)S(1)}, u32[]{:S(2)}, u32[]{:S(2)}) async-start(f32[16,56,128]{2,1,0:T(8,128)} %pad_maximum_fusion), calls=%async_computation | async-start | bytes 917504 | tf_op jit(solution)/shard_map/all_to_all | solution.py:279
  11.3 18.6 %copy-start.8 = (f32[768]{0:T(1024)S(1)}, f32[768]{0:T(1024)}, u32[]{:S(2)}) copy-start(f32[768]{0:T(1024)} %param.13) | copy-start | bytes 9220
  21.9 21.6 %all-to-all-start.1 = ((bf16[128,8,256]{2,1,0:T(8,128)(2,1)}), bf16[128,8,256]{2,1,0:T(8,128)(2,1)S(1)}, u32[]{:S(2)}, u32[]{:S(2)}) async-start(bf16[128,8,256]{2,1,0:T(8,128)(2,1)} %bitcast.4), calls=%async_computation.1 | async-start | bytes 1048576 | tf_op jit(solution)/shard_map/all_to_all | solution.py:285
  57.3 52.1 %copy-start.4 = (f32[32,768]{1,0:T(8,128)S(1)}, f32[32,768]{1,0:T(8,128)}, u32[]{:S(2)}) copy-start(f32[32,768]{1,0:T(8,128)} %param.12) | copy-start | bytes 294916
  57.3 52.6 %copy-start.3 = (f32[32,768]{1,0:T(8,128)S(1)}, f32[32,768]{1,0:T(8,128)}, u32[]{:S(2)}) copy-start(f32[32,768]{1,0:T(8,128)} %param.11) | copy-start | bytes 294916
  57.3 54.4 %copy-start.5 = (bf16[64,768]{1,0:T(8,128)(2,1)S(1)}, bf16[64,768]{1,0:T(8,128)(2,1)}, u32[]{:S(2)}) copy-start(bf16[64,768]{1,0:T(8,128)(2,1)} %param.10) | copy-start | bytes 294916
  103.1 26.2 %collective-permute-start = (bf16[128,96,128]{2,1,0:T(8,128)(2,1)S(1)}, bf16[128,96,128]{2,1,0:T(8,128)(2,1)}, u32[]{:S(2)}, u32[]{:S(2)}) collective-permute-start(bf16[128,96,128]{2,1,0:T(8,128)(2,1)S(1)} %all_to_all.20), channel_id=1, source_target_pairs={{0,1},{1,0},{2,3},{3,2},{4,5},{5,4},{6,7},{7,6},{8,9},{9,8},{10,11... | collective-permute-start | bytes 9437192 | tf_op jit(solution)/shard_map/ppermute | solution.py:299
  105.2 23.2 %all-to-all-start.3 = ((bf16[8,8,8,256]{3,2,1,0:T(8,128)(2,1)}), bf16[8,8,8,256]{3,2,1,0:T(8,128)(2,1)}, u32[]{:S(2)}, u32[]{:S(2)}) async-start(bf16[8,8,8,256]{3,2,1,0:T(8,128)(2,1)} %broadcast_in_dim.89), calls=%async_computation.3 | async-start | bytes 524288 | tf_op jit(solution)/shard_map/all_to_all | solution.py:288
  126.4 2.0 %copy-start.1 = (bf16[2048,1024]{1,0:T(8,128)(2,1)}, bf16[2048,1024]{1,0:T(8,128)(2,1)S(1)}, u32[]{:S(2)}) copy-start(bf16[2048,1024]{1,0:T(8,128)(2,1)S(1)} %inverse_table.1.inverse_ref) | copy-start | bytes 12582916
  129.4 1.4 copy-start
  130.8 2.2 %copy-start.2 = (bf16[2048,1024]{1,0:T(8,128)(2,1)S(1)}, bf16[2048,1024]{1,0:T(8,128)(2,1)}, u32[]{:S(2)}) copy-start(bf16[2048,1024]{1,0:T(8,128)(2,1)} %copy-done.1) | copy-start | bytes 12582916

commit v2 on v1

v2 whole, which is shorter than its diff:
```python
import math

import jax
import jax.numpy as jnp
from jax import lax
from jax.experimental import pallas as pl
from jax.experimental.pallas import tpu as pltpu
from jax.sharding import Mesh
from jax.sharding import PartitionSpec as P

NT = 16384
TOUT = 1024
BLOCK = 32
GROUP = 8
OWN = 4
TILE = 128
SLICE = 48
ALL = ("st", "z", "core")
FQ = ("z", "core")
MIB = 1 << 20

COS = (1.0, -19.739208221435547, 64.93939208984375, -85.45665740966797, 60.242130279541016,
       -26.4046688079834, 7.800131797790527, -1.4531123638153076)
SIN = (6.2831854820251465, -41.34170150756836, 81.60513305664062, -76.70301818847656,
       42.02592849731445, -14.899847984313965, 3.238137722015381)


def horner(terms, y):
    total = y * terms[-1] + terms[-2]
    for term in terms[-3::-1]:
        total = total * y + term
    return total


def cos_sin(turns):
    r = turns - jnp.floor(turns + 0.5)
    y = r * r
    return horner(COS, y), r * horner(SIN, y)


def table_turns(steps, bins):
    return ((steps * bins) & (NT - 1)).astype(jnp.float32) * (1.0 / NT)


def spectrum_kernel(
    fq_ref, signals_ref, bins_ref, gain_ref, damping_ref, damping_up_ref, places_ref,
    send_ref, spec_ref, windowed, tables,
):
    sensors = spec_ref.shape[1]
    slices = send_ref.shape[0]
    q = pl.program_id(0)
    coarse = lax.broadcasted_iota(jnp.int32, (128, 128), 0)
    fine = lax.broadcasted_iota(jnp.int32, (128, 128), 1)

    @pl.when(q == 0)
    def _():
        times = (coarse * 128 + fine).astype(jnp.float32)
        hann = 0.5 - 0.5 * cos_sin(times * (1.0 / NT))[0]
        for s in range(sensors):
            rows = pl.ds(s * 128, 128)
            windowed[rows, :] = (signals_ref[rows, :].astype(jnp.float32) * hann).astype(jnp.bfloat16)
        values = jnp.concatenate(
            [gain_ref[...].astype(jnp.float32), damping_ref[...], damping_up_ref[...]], axis=0
        ).T
        high = values.astype(jnp.bfloat16).astype(jnp.float32)
        rest = values - high
        middle = rest.astype(jnp.bfloat16).astype(jnp.float32)
        low = rest - middle
        tables[:, :SLICE, :128] = high.reshape(slices, SLICE, 128)
        tables[:, :SLICE, 128:] = (middle + pltpu.roll(low, 64, 1)).reshape(slices, SLICE, 128)
        tables[:, SLICE:, :] = jnp.zeros((slices, 64 - SLICE, 256), jnp.float32)
        for n in range(slices):
            tables[n, SLICE:SLICE + 8, :128] = places_ref[...]

    bins = bins_ref[pl.ds(q, 1), :]
    c1, s1 = cos_sin(table_turns(coarse, bins))
    table = jnp.concatenate(
        [(c1 * (1 / 128)).astype(jnp.bfloat16), (s1 * (-1 / 128)).astype(jnp.bfloat16)], axis=1
    )
    c2, s2 = cos_sin(table_turns(coarse * 128, bins))
    for s in range(sensors):
        part = jnp.dot(windowed[pl.ds(s * 128, 128), :], table, preferred_element_type=jnp.float32)
        re, im = part[:, :TILE], part[:, TILE:]
        spec_ref[0, s:s + 1, :TILE] = jnp.sum(re * c2 + im * s2, axis=0, keepdims=True)
        spec_ref[0, s:s + 1, TILE:] = jnp.sum(im * c2 - re * s2, axis=0, keepdims=True)
    own = spec_ref[0]
    rows = pl.ds(pl.multiple_of(fq_ref[0] * 8, 8), 8)
    for n in range(slices):
        send_ref[n, 0] = jnp.concatenate([own, tables[n, rows, :]], axis=0).astype(jnp.bfloat16)


def spectrum(fq, signals, freq_bins, gain, damping, damping_up, places, slices):
    sensors = signals.shape[0]
    tiles = freq_bins.shape[0] // TILE
    bins = freq_bins.reshape(tiles, TILE)
    whole = lambda a: pl.BlockSpec(a.shape, lambda q: (0, 0))
    signals = signals.reshape(sensors * 128, 128)
    return pl.pallas_call(
        spectrum_kernel,
        grid=(tiles,),
        in_specs=[
            pl.BlockSpec(memory_space=pltpu.SMEM),
            whole(signals),
            whole(bins),
            whole(gain),
            whole(damping),
            whole(damping_up),
            whole(places),
        ],
        out_specs=[
            pl.BlockSpec((slices, 1, 16, 2 * TILE), lambda q: (0, q, 0, 0)),
            pl.BlockSpec((1, sensors, 2 * TILE), lambda q: (q, 0, 0)),
        ],
        out_shape=[
            jax.ShapeDtypeStruct((slices, tiles, 16, 2 * TILE), jnp.bfloat16),
            jax.ShapeDtypeStruct((tiles, sensors, 2 * TILE), jnp.float32),
        ],
        scratch_shapes=[
            pltpu.VMEM((sensors * 128, 128), jnp.bfloat16),
            pltpu.VMEM((slices, 64, 2 * TILE), jnp.float32),
        ],
        compiler_params=pltpu.CompilerParams(vmem_limit_bytes=56 * MIB),
        cost_estimate=pl.CostEstimate(flops=2 * 10**9, bytes_accessed=10**6, transcendentals=0),
        name="spectrum",
    )(fq, signals, bins, gain, damping, damping_up, places)


def inverse_kernel(bins_ref, after_ref, out_ref):
    del after_ref
    bins = bins_ref[:, 0:1]
    lane = lax.broadcasted_iota(jnp.int32, (TILE, 128), 1)
    c1, s1 = cos_sin(table_turns(lane, bins))
    c2, s2 = cos_sin(table_turns(lane * 128 + (NT - TOUT), bins))
    c2, s2 = c2 * (1 / 32), s2 * (1 / 32)
    for n in range(TOUT // 128):
        c, s = c2[:, n:n + 1], s2[:, n:n + 1]
        columns = pl.ds(n * 128, 128)
        out_ref[:TILE, columns] = (c1 * c - s1 * s).astype(jnp.bfloat16)
        out_ref[TILE:, columns] = (-s1 * c - c1 * s).astype(jnp.bfloat16)


def inverse_table(freq_bins, after):
    tiles = freq_bins.shape[0] // TILE
    bins = jnp.broadcast_to(freq_bins[:, None], (tiles * TILE, 128))
    return pl.pallas_call(
        inverse_kernel,
        grid=(tiles,),
        in_specs=[
            pl.BlockSpec((TILE, 128), lambda q: (q, 0)),
            pl.BlockSpec(memory_space=pl.ANY),
        ],
        out_specs=pl.BlockSpec((2 * TILE, TOUT), lambda q: (q, 0)),
        out_shape=jax.ShapeDtypeStruct((tiles * 2 * TILE, TOUT), jnp.bfloat16),
        compiler_params=pltpu.CompilerParams(vmem_limit_bytes=56 * MIB),
        cost_estimate=pl.CostEstimate(flops=4 * 10**9, bytes_accessed=5 * 10**6, transcendentals=0),
        name="inverse_table",
    )(bins, after)


def turn(c, s, re, im):
    return c * re - s * im, c * im + s * re


def turn_back(c, s, re, im):
    return c * re + s * im, c * im - s * re


def step(rate, turned, f_re, f_im):
    return rate * turned[0] + f_re, rate * turned[1] + f_im


def march_kernel(recv_ref, rot_ref, out_ref, done_ref, force):
    done_ref[...] = jnp.zeros_like(done_ref)
    tiles = 8
    blocks = recv_ref.shape[0] // tiles

    def table_rows(block, p):
        return recv_ref[block * tiles + p].astype(jnp.float32)[8:]

    def forcing(block, stations, slot):
        gain = jnp.concatenate([table_rows(block, p) for p in range(SLICE // 8)], axis=0)[:, :64]
        local = table_rows(block, SLICE // 8)[0:1, :64]
        spec = jnp.concatenate(
            [recv_ref[block * tiles + p].astype(jnp.float32)[:8] for p in range(tiles)], axis=0
        ).astype(jnp.bfloat16)
        chosen = jnp.concatenate(
            [jnp.where(local == jnp.float32(k), gain, 0.0) for k in stations], axis=0
        ).astype(jnp.bfloat16)
        slot[...] = jnp.dot(chosen, spec, preferred_element_type=jnp.float32)

    def rates_of(block):
        both = jnp.concatenate([table_rows(block, p) for p in range(SLICE // 8)], axis=0)
        rest = both[:, 128:]
        return both[:, :128] + rest + pltpu.roll(rest, 64, 1)

    chunks = BLOCK // GROUP
    down_of = [range(n * GROUP, n * GROUP + GROUP) for n in range(chunks)]
    up_of = [range(BLOCK - 1 - n * GROUP, BLOCK - 1 - n * GROUP - GROUP, -1) for n in range(chunks)]

    def body(b, carry):
        d_re, d_im, u_re, u_im = carry
        up = blocks - 1 - b
        c, s = rot_ref[0], rot_ref[1]
        down_rates = rates_of(b)
        up_rates = rates_of(up)
        for n in range(chunks):
            now, later = n % 2, (n + 1) % 2
            if n + 1 < chunks:
                forcing(b, down_of[n + 1], force.at[later, 0])
                forcing(up, up_of[n + 1], force.at[later, 1])
            else:
                forcing(jnp.minimum(b + 1, blocks - 1), down_of[0], force.at[later, 0])
                forcing(jnp.maximum(up - 1, 0), up_of[0], force.at[later, 1])
            group = 2 * (b * chunks + n)
            out_ref[group, :SLICE, :] = d_re.astype(jnp.bfloat16)
            out_ref[group, SLICE:, :] = d_im.astype(jnp.bfloat16)
            group = 2 * (up * chunks + chunks - 1 - n) + 1
            out_ref[group, :SLICE, :] = u_re.astype(jnp.bfloat16)
            out_ref[group, SLICE:, :] = u_im.astype(jnp.bfloat16)
            for i in range(GROUP):
                rows = pl.ds(i * SLICE, SLICE)
                k, j = down_of[n][i], up_of[n][i]
                d_re, d_im = step(
                    down_rates[:, 64 + k:65 + k], turn_back(c, s, d_re, d_im),
                    force[now, 0, rows, :TILE], force[now, 0, rows, TILE:],
                )
                u_re, u_im = step(
                    up_rates[:, 96 + j:97 + j], turn(c, s, u_re, u_im),
                    force[now, 1, rows, :TILE], force[now, 1, rows, TILE:],
                )
        return d_re, d_im, u_re, u_im

    forcing(0, down_of[0], force.at[0, 0])
    forcing(blocks - 1, up_of[0], force.at[0, 1])
    zero = jnp.zeros((SLICE, TILE), jnp.float32)
    lax.fori_loop(0, blocks, body, (zero, zero, zero, zero))


def entering_states(recv, rot, blocks):
    return pl.pallas_call(
        march_kernel,
        out_shape=[
            jax.ShapeDtypeStruct((2 * blocks * BLOCK // GROUP, 2 * SLICE, TILE), jnp.bfloat16),
            jax.ShapeDtypeStruct((8, 128), jnp.float32),
        ],
        in_specs=[pl.BlockSpec(memory_space=pltpu.VMEM)] * 2,
        out_specs=[pl.BlockSpec(memory_space=pltpu.VMEM)] * 2,
        scratch_shapes=[pltpu.VMEM((2, 2, GROUP * SLICE, 2 * TILE), jnp.float32)],
        compiler_params=pltpu.CompilerParams(vmem_limit_bytes=56 * MIB),
        cost_estimate=pl.CostEstimate(flops=12 * 10**9, bytes_accessed=5 * 10**6, transcendentals=0),
        name="entering_states",
    )(recv, rot)


TURN = GROUP + OWN
SKIP = TURN + 1


def local_kernel(gain_ref, rates_ref, spec_ref, omega_ref, after_ref, part_ref, rot_ref, force, kept):
    del after_ref
    pair = force.shape[0]
    rates = rates_ref[0]

    def two(n, unused):
        for p in range(pair):
            q = n * pair + p
            force[p] = jnp.dot(gain_ref[0], spec_ref[q], preferred_element_type=jnp.float32)
        for p in range(pair):
            q = n * pair + p

            def forced(i):
                rows = pl.ds(i * SLICE, SLICE)
                return force[p, rows, :TILE], force[p, rows, TILE:]

            c, s = cos_sin(omega_ref[q, 0:1, :] * rates[:, TURN:TURN + 1])
            rot_ref[0, q, :SLICE, :] = c
            rot_ref[0, q, SLICE:, :] = s
            re, im = forced(GROUP - 1)
            kept[p, 0, 0], kept[p, 0, 1] = re, im
            for i in range(1, OWN):
                re, im = step(
                    rates[:, GROUP + i:GROUP + i + 1], turn_back(c, s, re, im),
                    *forced(GROUP - 1 - i),
                )
                kept[p, i, 0], kept[p, i, 1] = re, im
            re, im = forced(0)
            for i in range(1, GROUP):
                re, im = step(rates[:, i:i + 1], turn(c, s, re, im), *forced(i))
                if i >= GROUP - OWN:
                    n_own, n_near = i - (GROUP - OWN), GROUP - 1 - i
                    part_ref[0, q, n_own, :SLICE, :] = (re + kept[p, n_near, 0]).astype(jnp.bfloat16)
                    part_ref[0, q, n_own, SLICE:, :] = (im + kept[p, n_near, 1]).astype(jnp.bfloat16)
        return unused

    lax.fori_loop(0, spec_ref.shape[0] // pair, two, 0)


def local_states(gain, rates, spec, omega, after):
    slices, tiles = gain.shape[0], spec.shape[0]
    whole = lambda a: pl.BlockSpec(a.shape, lambda t: (0,) * a.ndim)
    return pl.pallas_call(
        local_kernel,
        grid=(slices,),
        in_specs=[
            pl.BlockSpec((1, GROUP * SLICE, 64), lambda t: (t, 0, 0)),
            pl.BlockSpec((1, SLICE, 128), lambda t: (t, 0, 0)),
            whole(spec),
            whole(omega),
            pl.BlockSpec(memory_space=pl.ANY),
        ],
        out_specs=[
            pl.BlockSpec((1, tiles, OWN, 2 * SLICE, TILE), lambda t: (t, 0, 0, 0, 0)),
            pl.BlockSpec((1, tiles, 2 * SLICE, TILE), lambda t: (t, 0, 0, 0)),
        ],
        out_shape=[
            jax.ShapeDtypeStruct((slices, tiles, OWN, 2 * SLICE, TILE), jnp.bfloat16),
            jax.ShapeDtypeStruct((slices, tiles, 2 * SLICE, TILE), jnp.float32),
        ],
        scratch_shapes=[
            pltpu.VMEM((2, GROUP * SLICE, 2 * TILE), jnp.float32),
            pltpu.VMEM((2, OWN, 2, SLICE, TILE), jnp.float32),
        ],
        compiler_params=pltpu.CompilerParams(vmem_limit_bytes=56 * MIB),
        cost_estimate=pl.CostEstimate(flops=20 * 10**9, bytes_accessed=20 * 10**6, transcendentals=0),
        name="local_states",
    )(gain, rates, spec, omega, after)


def estimate_kernel(
    core_ref, near_ref, far_ref, part_ref, rot_ref, rates_ref, inverse_ref, out_ref, even, odd, kept
):
    per, tiles = near_ref.shape[:2]
    height = per * SLICE
    index, last = pl.program_id(0), pl.num_programs(0) - 1
    core = core_ref[0]
    pieces = TOUT // 256

    def fill(state, q):
        lane = pl.multiple_of(q * 2 * TILE, 2 * TILE)
        for t in range(per):
            rates = rates_ref[t]
            c, s = rot_ref[t, q, :SLICE, :], rot_ref[t, q, SLICE:, :]
            re = near_ref[t, q, :SLICE, :].astype(jnp.float32)
            im = near_ref[t, q, SLICE:, :].astype(jnp.float32)
            for i in range(OWN):
                rate = rates[:, GROUP + i:GROUP + i + 1]
                re, im = turn_back(c, s, re, im)
                re, im = rate * re, rate * im
                kept[t, i, 0], kept[t, i, 1] = re, im
            c4, s4 = turn(c, s, c, s)
            c4, s4 = turn(c4, s4, c4, s4)
            re = far_ref[t, q, :SLICE, :].astype(jnp.float32)
            im = far_ref[t, q, SLICE:, :].astype(jnp.float32)
            re, im = turn(c4, s4, re, im)
            skip = rates[:, SKIP:SKIP + 1]
            re, im = skip * re, skip * im
            for i in range(OWN):
                rate = rates[:, GROUP - OWN + i:GROUP - OWN + i + 1]
                re, im = turn(c, s, re, im)
                re, im = rate * re, rate * im
                n = OWN - 1 - i
                own = jnp.where(core == 0, n, i)
                rows = pl.ds(t * SLICE, SLICE)
                whole_re = re + kept[t, n, 0] + part_ref[t, q, i, :SLICE, :].astype(jnp.float32)
                whole_im = im + kept[t, n, 1] + part_ref[t, q, i, SLICE:, :].astype(jnp.float32)
                state[own, rows, pl.ds(lane, TILE)] = whole_re.astype(jnp.bfloat16)
                state[own, rows, pl.ds(lane + TILE, TILE)] = whole_im.astype(jnp.bfloat16)

    def multiply(state, n):
        columns = pl.ds(pl.multiple_of(n * 256, 256), 256)
        out = jnp.dot(
            state[...].reshape(OWN * height, 2 * tiles * TILE), inverse_ref[:, columns],
            preferred_element_type=jnp.float32,
        )
        out_ref[:, :, columns] = out.astype(jnp.bfloat16).reshape(OWN, height, 256)

    def both(filled, multiplied):
        def piece(n, unused):
            if multiplied is not None:
                multiply(multiplied, n)
            if filled is not None:
                for p in range(tiles // pieces):
                    fill(filled, n * (tiles // pieces) + p)
            return unused

        lax.fori_loop(0, pieces, piece, 0)

    inner = (index > 0) & (index < last)
    pl.when(index == 0)(lambda: both(even, None))
    pl.when(inner & (index % 2 == 1))(lambda: both(odd, even))
    pl.when(inner & (index % 2 == 0))(lambda: both(even, odd))
    pl.when(index == last)(lambda: both(None, odd))


def estimates(core, near, far, part, rot, rates, inverse):
    slices, tiles = near.shape[:2]
    per = 4
    steps = slices // per
    assert steps % 2 == 0
    here = lambda i: jnp.minimum(i, steps - 1)
    return pl.pallas_call(
        estimate_kernel,
        grid=(steps + 1,),
        in_specs=[
            pl.BlockSpec(memory_space=pltpu.SMEM),
            pl.BlockSpec((per, tiles, 2 * SLICE, TILE), lambda i: (here(i), 0, 0, 0)),
            pl.BlockSpec((per, tiles, 2 * SLICE, TILE), lambda i: (here(i), 0, 0, 0)),
            pl.BlockSpec((per, tiles, OWN, 2 * SLICE, TILE), lambda i: (here(i), 0, 0, 0, 0)),
            pl.BlockSpec((per, tiles, 2 * SLICE, TILE), lambda i: (here(i), 0, 0, 0)),
            pl.BlockSpec((per, SLICE, 128), lambda i: (here(i), 0, 0)),
            pl.BlockSpec(inverse.shape, lambda i: (0, 0), pipeline_mode=pl.Buffered(1)),
        ],
        out_specs=pl.BlockSpec((OWN, per * SLICE, TOUT), lambda i: (0, jnp.maximum(i - 1, 0), 0)),
        out_shape=jax.ShapeDtypeStruct((OWN, slices * SLICE, TOUT), jnp.bfloat16),
        scratch_shapes=[
            pltpu.VMEM((OWN, per * SLICE, 2 * tiles * TILE), jnp.bfloat16),
            pltpu.VMEM((OWN, per * SLICE, 2 * tiles * TILE), jnp.bfloat16),
            pltpu.VMEM((per, OWN, 2, SLICE, TILE), jnp.float32),
        ],
        compiler_params=pltpu.CompilerParams(vmem_limit_bytes=40 * MIB),
        cost_estimate=pl.CostEstimate(flops=20 * 10**9, bytes_accessed=40 * 10**6, transcendentals=0),
        name="estimates",
    )(core, near, far, part, rot, rates, inverse)


def on_device(signals, freq_bins, sensor_station, gain, damping, damping_up, phase_speed):
    st, z, core = (lax.axis_index(axis) for axis in ALL)
    blocks = lax.axis_size("st")
    tiles = freq_bins.shape[0] // TILE
    sensors = sensor_station.shape[0]
    local = sensor_station - st * BLOCK
    places = jnp.broadcast_to(jnp.pad(local.astype(jnp.float32), (0, 128 - sensors)), (8, 128))

    fq = (z * 2 + core).astype(jnp.int32)
    send, spec = spectrum(fq.reshape(1), signals, freq_bins, gain, damping, damping_up, places, blocks)
    send = send.reshape((blocks * tiles,) + send.shape[2:])
    recv = lax.all_to_all(send, ALL, split_axis=0, concat_axis=0, tiled=True)
    to_fq = jnp.broadcast_to(spec.astype(jnp.bfloat16)[None], (tiles,) + spec.shape)
    spec_block = lax.all_to_all(to_fq, FQ, split_axis=0, concat_axis=0, tiled=True)
    spec_block = spec_block.transpose(1, 0, 2, 3).reshape(tiles, sensors, 2 * TILE)

    omega = (freq_bins.astype(jnp.float32) / NT).reshape(tiles, 1, TILE)
    own_omega = lax.dynamic_index_in_dim(omega, fq, 0, keepdims=False)
    own_speed = lax.dynamic_slice_in_dim(phase_speed, st * SLICE, SLICE)
    theta = 2 * math.pi * own_omega * own_speed[:, None]
    rot = jnp.stack([jnp.cos(theta), jnp.sin(theta)])
    entering, done = entering_states(recv, rot, blocks)
    near = lax.all_to_all(entering, ALL, split_axis=0, concat_axis=0, tiled=True)

    first = z * GROUP
    down = lax.dynamic_slice_in_dim(damping, first, GROUP)
    up = lax.dynamic_slice_in_dim(damping_up, first, GROUP)[::-1]
    far_rates = jnp.where(core == 0, up, down)
    near_rates = jnp.where(core == 0, down, up)[:OWN]
    speed = jnp.where(core == 0, phase_speed, -phase_speed)[None]
    skip = jnp.prod(far_rates[:GROUP - OWN], axis=0, keepdims=True)
    rates = jnp.concatenate([far_rates, near_rates, speed, skip], axis=0)
    rates = jnp.pad(rates, ((0, 128 - rates.shape[0]), (0, 0))).T.reshape(blocks, SLICE, 128)
    eight = lax.iota(jnp.int32, GROUP)
    far_order = first + jnp.where(core == 0, GROUP - 1 - eight, eight)
    at = (local[None, :] == far_order[:, None])[None, :, None, :]
    own_gain = jnp.where(at, gain.T.reshape(blocks, 1, SLICE, sensors), 0)
    own_gain = own_gain.reshape(blocks, GROUP * SLICE, sensors)

    part, turns = local_states(
        own_gain, rates, spec_block, jnp.broadcast_to(omega, (tiles, 8, TILE)), done
    )
    inverse = inverse_table(freq_bins, done)
    near, part, turns, inverse = lax.optimization_barrier((near, part, turns, inverse))
    far = lax.ppermute(near, "core", [(0, 1), (1, 0)])
    shape = (blocks, tiles, 2 * SLICE, TILE)
    return estimates(
        core.reshape(1).astype(jnp.int32), near.reshape(shape), far.reshape(shape), part, turns,
        rates, inverse,
    )


def solution(mesh):
    torus = Mesh(mesh.devices.reshape(mesh.shape["st"], 4, 2), ALL)
    placed = (P(ALL, None), P(), P("st"), P("st", None), P("st", None), P("st", None), P())
    return jax.shard_map(
        on_device, mesh=torus, in_specs=placed, out_specs=P(ALL, None, None), check_vma=False
    )
```

time: 177 us -> 151 us (0.85)
  blocking collectives: 45.8 us -> 0 us
  Pallas kernels: 70.2 us -> 86.7 us
    all_to_all x1 -> x0, blocking collectives: 45.8 us -> none  [on_device(): lax.all_to_all(entering, ALL, split_axis=0, concat_axis=0, tiled=True)]
    pallas_call x3 -> x4, Pallas kernels: 60.9 us -> 79.3 us  [the longest x1 29.8 us: estimates(): pl.pallas_call(estimate_kernel, grid=(steps + 1,), in_specs=[pl.BlockSpec...]
    ppermute x1, waiting for transfers between devices: 0.01 us -> 5.29 us  [on_device(): far = lax.ppermute(near, 'core', [(0, 1), (1, 0)])]
    all_to_all x2, waiting for transfers between devices: 19.4 us -> 15 us  [the longest x1 14.9 us: on_device(): recv = lax.all_to_all(send, ALL, split_axis=0, concat_axis=0, tiled=True)]
    unnamed x18 -> x16, local copies, waits for them, and re-layouts: 5.63 us -> 2.91 us
    gather x4 -> x0, local copies, waits for them, and re-layouts: 2.27 us -> none  [the longest x2 1.13 us: on_device(): far_rates = jnp.where(core == 0, damping_up[far_order], damping[far_order])]
    pallas_call x1, Pallas kernels: 9.35 us -> 7.31 us  [inverse_table(): pl.pallas_call(inverse_kernel, grid=(tiles,), in_specs=[pl.BlockSpec((TIL...]
    select_n x6 -> x4, other arithmetic: 2.24 us -> 3.71 us  [the longest x1 2.21 us: on_device(): own_gain = jnp.where(at, gain.T.reshape(blocks, 1, SLICE, sensors), 0)]
  transfers between devices with their start and end apart: 4 -> 4, of which waited for: 2 -> 2; matrix products, arithmetic and copies ran while one was open for 6% -> 9% of each run, Pallas kernels for 7% -> 34%
where the time goes in v2:
time: 151 us; the launch traced here: 149 us
  Pallas kernels  86.7 us (57%)
  starting transfers between devices  22.2 us (15%)
  waiting for transfers between devices  20.2 us (13%)
  local copies, waits for them, and re-layouts  12 us (8%)
  other arithmetic  8.13 us (5%)
    pallas_call x1, Pallas kernels, estimates(): pl.pallas_call(estimate_kernel, grid=(steps + 1,), in_specs=[pl.BlockSpec...  29.8 us
    pallas_call x1, Pallas kernels, local_states(): pl.pallas_call(local_kernel, grid=(slices,), in_specs=[pl.BlockSpec((1, G...  25.8 us
    pallas_call x1, Pallas kernels, entering_states(): pl.pallas_call(march_kernel, out_shape=[jax.ShapeDtypeStruct((2 * blocks...  17.4 us
    all_to_all x1, waiting for transfers between devices, on_device(): recv = lax.all_to_all(send, ALL, split_axis=0, concat_axis=0, tiled=True)  14.9 us
    all_to_all x1, starting transfers between devices, on_device(): recv = lax.all_to_all(send, ALL, split_axis=0, concat_axis=0, tiled=True)  11.5 us
    pallas_call x1, Pallas kernels, inverse_table(): pl.pallas_call(inverse_kernel, grid=(tiles,), in_specs=[pl.BlockSpec((TIL...  7.31 us
    pallas_call x1, Pallas kernels, spectrum(): pl.pallas_call(spectrum_kernel, grid=(tiles,), in_specs=[pl.BlockSpec(mem...  6.29 us
    ppermute x1, waiting for transfers between devices, on_device(): far = lax.ppermute(near, 'core', [(0, 1), (1, 0)])  5.29 us
  transfers between devices with their start and end apart: 4, of which 2 were waited for; matrix products, arithmetic and copies ran while one was open for 9% of the time, Pallas kernels for 34%

profile of v2, /device:TPU:1, one launch (start us, length us, event | category | flops | bytes accessed | tf_op | source)
XLA Modules:
  0.0 149.4 jit_solution(14132473055000279060)
XLA Ops:
  0.0 1.8 %reshape.167.signals_ref = bf16[1024,128]{1,0:T(8,128)(2,1)} reshape(bf16[8,16384]{1,0:T(8,128)(2,1)} %param.7) | data formatting | bytes 524288 | tf_op jit(solution)/shard_map/reshape | solution.py:97
  1.8 1.2 fusion.5
  3.0 0.6 broadcast_in_dim.60.places_ref
  3.6 0.0 copy-start.7
  3.6 0.0 copy-start.5
  3.6 0.0 copy-start.6
  3.6 6.3 %spectrum.1 = (bf16[16,8,16,256]{3,2,1,0:T(8,128)(2,1)}, f32[8,8,256]{2,1,0:T(8,128)}) custom-call(s32[1]{0:T(128)} %bitcast.1.fq_ref, bf16[1024,128]{1,0:T(8,128)(2,1)} %reshape.167.signals_ref, s32[8,128]{1,0:T(8,128)} %bitcast.32, bf16[64,768]{1,0:T(8,128)(2,1)} %gain_ref.1, f32[32,768]{1,0:T(8,128)} %damping_ref.1, f32[32,768]{1,0:T(8,128)} %damping_up_ref.1, ...), custom_call_target="tpu_custom_call" | custom-call | flops 2000000000 | bytes 1000000 | tf_op jit(solution)/shard_map/spectrum/pallas_call | solution.py:98
  9.9 11.5 %all-to-all-start = ((bf16[128,16,256]{2,1,0:T(8,128)(2,1)}), bf16[128,16,256]{2,1,0:T(8,128)(2,1)S(1)}, u32[]{:S(2)}, u32[]{:S(2)}) async-start(bf16[128,16,256]{2,1,0:T(8,128)(2,1)} %bitcast.28), calls=%async_computation | async-start | bytes 2097152 | tf_op jit(solution)/shard_map/all_to_all | solution.py:437
  21.4 0.0 copy-done.7
  21.5 0.7 constant_dynamic-slice_fusion
  22.2 0.1 dynamic_slice.14
  22.3 0.1 rev.3
  22.4 0.7 dynamic-slice_select_fusion
  23.1 0.0 copy-start.4
  23.2 0.0 copy-done.5
  23.2 0.8 copy.15
  24.0 0.8 convert_element_type.17
  24.8 0.0 copy-done.6
  24.9 0.2 multiply_cosine_fusion
  25.0 0.6 pad_maximum_fusion.rot_ref
  25.6 14.9 %all-to-all-done.recv_ref = bf16[128,16,256]{2,1,0:T(8,128)(2,1)S(1)} async-done(((bf16[128,16,256]{2,1,0:T(8,128)(2,1)}), bf16[128,16,256]{2,1,0:T(8,128)(2,1)S(1)}, u32[]{:S(2)}, u32[]{:S(2)}) %all-to-all-start) | async-done | bytes 1048608 | tf_op jit(solution)/shard_map/all_to_all | solution.py:437
  40.6 0.0 copy-start.2
  40.6 0.8 broadcast_in_dim.70
  41.4 0.0 copy-done.4
  41.4 4.5 %all-to-all-start.2 = ((bf16[8,8,8,256]{3,2,1,0:T(8,128)(2,1)}), bf16[8,8,8,256]{3,2,1,0:T(8,128)(2,1)S(1)}, u32[]{:S(2)}, u32[]{:S(2)}) async-start(bf16[8,8,8,256]{3,2,1,0:T(8,128)(2,1)} %broadcast_in_dim.70), calls=%async_computation.2 | async-start | bytes 524288 | tf_op jit(solution)/shard_map/all_to_all | solution.py:439
  45.9 0.0 copy-done.2
  45.9 17.4 %entering_states.1 = (bf16[128,96,128]{2,1,0:T(8,128)(2,1)}, f32[8,128]{1,0:T(8,128)}) custom-call(bf16[128,16,256]{2,1,0:T(8,128)(2,1)} %copy-done.2, f32[2,48,128]{2,1,0:T(8,128)} %pad_maximum_fusion.rot_ref), custom_call_target="tpu_custom_call" | custom-call | flops 12000000000 | bytes 5000000 | tf_op jit(solution)/shard_map/entering_states/pallas_call | solution.py:240
  63.3 0.0 all-to-all-done.2
  63.3 0.0 copy-start.3
  63.3 0.7 copy-done.3
  64.0 5.1 %all-to-all-start.1 = ((bf16[128,96,128]{2,1,0:T(8,128)(2,1)}), bf16[128,96,128]{2,1,0:T(8,128)(2,1)S(1)}, u32[]{:S(2)}, u32[]{:S(2)}) async-start(bf16[128,96,128]{2,1,0:T(8,128)(2,1)} %get-tuple-element.16), calls=%async_computation.1 | async-start | bytes 6291456 | tf_op jit(solution)/shard_map/all_to_all | solution.py:448
  69.1 0.8 slice_select_fusion
  69.9 0.8 fusion
  70.7 0.9 copy.13
  71.6 0.8 broadcast_compare_fusion
  72.4 2.2 %bitcast_select_fusion.gain_ref = bf16[16,384,64]{2,1,0:T(8,128)(2,1)} fusion(pred[384,64]{1,0:T(8,128)(4,1)S(1)} %bitcast.30, bf16[16,48,64]{2,1,0:T(8,128)(2,1)} %bitcast.29), kind=kLoop, calls=%fused_computation | loop fusion | flops 393216 | bytes 909312 | tf_op jit(solution)/shard_map/jit(_where)/select_n | solution.py:462
  74.6 1.7 %copy_bitcast_fusion.spec_ref = bf16[8,64,256]{2,1,0:T(8,128)(2,1)} fusion(bf16[8,8,8,256]{3,2,1,0:T(8,128)(2,1)} %copy-done.3), kind=kLoop, calls=%fused_computation.6 | loop fusion | bytes 524288 | tf_op jit(solution)/shard_map/reshape | solution.py:440
  76.2 1.0 broadcast_in_dim.73.bins_ref
  77.2 7.3 %inverse_table.1.inverse_ref = bf16[2048,1024]{1,0:T(8,128)(2,1)} custom-call(s32[1024,128]{1,0:T(8,128)} %broadcast_in_dim.73.bins_ref, f32[8,128]{1,0:T(8,128)} %get-tuple-element.18.after_ref), custom_call_target="tpu_custom_call" | custom-call | flops 4000000000 | bytes 5000000 | tf_op jit(solution)/shard_map/inverse_table/pallas_call | solution.py:145
  84.6 0.6 broadcast_in_dim.72.omega_ref
  85.2 0.0 copy-start
  85.2 25.8 %local_states.1 = (bf16[16,8,4,96,128]{4,3,2,1,0:T(8,128)(2,1)}, f32[16,8,96,128]{3,2,1,0:T(8,128)}) custom-call(bf16[16,384,64]{2,1,0:T(8,128)(2,1)} %bitcast_select_fusion.gain_ref, f32[16,48,128]{2,1,0:T(8,128)} %bitcast.25, bf16[8,64,256]{2,1,0:T(8,128)(2,1)} %copy_bitcast_fusion.spec_ref, f32[8,8,128]{2,1,0:T(8,128)} %broadcast_in_dim.72.omega_ref, ...), custom_call_target="tpu_custom_call" | custom-call | flops 20000000000 | bytes 20000000 | tf_op jit(solution)/shard_map/local_states/pallas_call | solution.py:301
  111.0 0.0 all-to-all-done.1
  111.0 1.1 collective-permute-start
  112.1 5.3 %collective-permute-done = bf16[128,96,128]{2,1,0:T(8,128)(2,1)S(1)} collective-permute-done((bf16[128,96,128]{2,1,0:T(8,128)(2,1)S(1)}, bf16[128,96,128]{2,1,0:T(8,128)(2,1)S(1)}, u32[]{:S(2)}, u32[]{:S(2)}) %collective-permute-start) | collective-permute-done | bytes 3145760 | tf_op jit(solution)/shard_map/ppermute | solution.py:470
  117.4 0.0 copy-done
  117.4 0.0 copy-start.1
  117.4 2.2 %copy-done.1 = bf16[2048,1024]{1,0:T(8,128)(2,1)S(1)} copy-done((bf16[2048,1024]{1,0:T(8,128)(2,1)S(1)}, bf16[2048,1024]{1,0:T(8,128)(2,1)}, u32[]{:S(2)}) %copy-start.1) | copy-done | bytes 4194328
  119.6 29.8 %estimates.1 = bf16[4,768,1024]{2,1,0:T(8,128)(2,1)} custom-call(s32[1]{0:T(128)} %bitcast.core_ref, bf16[16,8,96,128]{3,2,1,0:T(8,128)(2,1)S(1)} %bitcast.24, bf16[16,8,96,128]{3,2,1,0:T(8,128)(2,1)S(1)} %bitcast.27, bf16[16,8,4,96,128]{4,3,2,1,0:T(8,128)(2,1)} %get-tuple-element.22.part_ref, f32[16,8,96,128]{3,2,1,0:T(8,128)} %get-tuple-element.23.rot_ref, ...), custom_call_target="tpu_custom_call" | custom-call | flops 20000000000 | bytes 40000000 | tf_op jit(solution)/shard_map/estimates/pallas_call | solution.py:401
  (9 shorter events, 0.1 us)
Async XLA Ops:
  3.6 17.8 %copy-start.7 = (f32[768]{0:T(1024)S(1)}, f32[768]{0:T(1024)}, u32[]{:S(2)}) copy-start(f32[768]{0:T(1024)} %param.13) | copy-start | bytes 9220
  3.6 19.5 %copy-start.5 = (bf16[64,768]{1,0:T(8,128)(2,1)S(1)}, bf16[64,768]{1,0:T(8,128)(2,1)}, u32[]{:S(2)}) copy-start(bf16[64,768]{1,0:T(8,128)(2,1)} %gain_ref.1) | copy-start | bytes 294916
  3.6 21.2 %copy-start.6 = (s32[1024]{0:T(1024)S(1)}, s32[1024]{0:T(1024)}, u32[]{:S(2)}) copy-start(s32[1024]{0:T(1024)} %param.8) | copy-start | bytes 12292
  9.9 30.7 %all-to-all-start = ((bf16[128,16,256]{2,1,0:T(8,128)(2,1)}), bf16[128,16,256]{2,1,0:T(8,128)(2,1)S(1)}, u32[]{:S(2)}, u32[]{:S(2)}) async-start(bf16[128,16,256]{2,1,0:T(8,128)(2,1)} %bitcast.28), calls=%async_computation | async-start | bytes 2097152 | tf_op jit(solution)/shard_map/all_to_all | solution.py:437
  23.1 18.3 %copy-start.4 = (f32[8,768]{1,0:T(8,128)}, f32[8,768]{1,0:T(8,128)S(1)}, u32[]{:S(2)}) copy-start(f32[8,768]{1,0:T(8,128)S(1)} %dynamic-slice_select_fusion) | copy-start | bytes 73732
  40.6 5.3 %copy-start.2 = (bf16[128,16,256]{2,1,0:T(8,128)(2,1)}, bf16[128,16,256]{2,1,0:T(8,128)(2,1)S(1)}, u32[]{:S(2)}) copy-start(bf16[128,16,256]{2,1,0:T(8,128)(2,1)S(1)} %all-to-all-done.recv_ref) | copy-start | bytes 3145732
  41.4 22.0 %all-to-all-start.2 = ((bf16[8,8,8,256]{3,2,1,0:T(8,128)(2,1)}), bf16[8,8,8,256]{3,2,1,0:T(8,128)(2,1)S(1)}, u32[]{:S(2)}, u32[]{:S(2)}) async-start(bf16[8,8,8,256]{3,2,1,0:T(8,128)(2,1)} %broadcast_in_dim.70), calls=%async_computation.2 | async-start | bytes 524288 | tf_op jit(solution)/shard_map/all_to_all | solution.py:439
  63.3 0.7 copy-start.3
  64.0 46.9 %all-to-all-start.1 = ((bf16[128,96,128]{2,1,0:T(8,128)(2,1)}), bf16[128,96,128]{2,1,0:T(8,128)(2,1)S(1)}, u32[]{:S(2)}, u32[]{:S(2)}) async-start(bf16[128,96,128]{2,1,0:T(8,128)(2,1)} %get-tuple-element.16), calls=%async_computation.1 | async-start | bytes 6291456 | tf_op jit(solution)/shard_map/all_to_all | solution.py:448
  85.2 32.2 %copy-start = (f32[768,128]{1,0:T(8,128)S(1)}, f32[768,128]{1,0:T(8,128)}, u32[]{:S(2)}) copy-start(f32[768,128]{1,0:T(8,128)} %copy.13) | copy-start | bytes 1179652
  111.0 6.4 %collective-permute-start = (bf16[128,96,128]{2,1,0:T(8,128)(2,1)S(1)}, bf16[128,96,128]{2,1,0:T(8,128)(2,1)S(1)}, u32[]{:S(2)}, u32[]{:S(2)}) collective-permute-start(bf16[128,96,128]{2,1,0:T(8,128)(2,1)S(1)} %all-to-all-done.1), channel_id=1, source_target_pairs={{0,1},{1,0},{2,3},{3,2},{4,5},{5,4},{6,7},{7,6},{8,9},{9,8},{10,11... | collective-permute-start | bytes 9437192 | tf_op jit(solution)/shard_map/ppermute | solution.py:470
  117.4 2.2 %copy-start.1 = (bf16[2048,1024]{1,0:T(8,128)(2,1)S(1)}, bf16[2048,1024]{1,0:T(8,128)(2,1)}, u32[]{:S(2)}) copy-start(bf16[2048,1024]{1,0:T(8,128)(2,1)} %inverse_table.1.inverse_ref) | copy-start | bytes 12582916

commit v3 on v2

v3 whole, which is shorter than its diff:
```python
import functools
import math

import jax
import jax.numpy as jnp
from jax import lax
from jax.experimental import pallas as pl
from jax.experimental.pallas import tpu as pltpu
from jax.sharding import Mesh
from jax.sharding import PartitionSpec as P

NT = 16384
TOUT = 1024
BLOCK = 32
GROUP = 8
OWN = 4
TILE = 128
SLICE = 48
ALL = ("st", "z", "core")
FQ = ("z", "core")
MIB = 1 << 20

COS = (1.0, -19.739208221435547, 64.93939208984375, -85.45665740966797, 60.242130279541016,
       -26.4046688079834, 7.800131797790527, -1.4531123638153076)
SIN = (6.2831854820251465, -41.34170150756836, 81.60513305664062, -76.70301818847656,
       42.02592849731445, -14.899847984313965, 3.238137722015381)


def horner(terms, y):
    total = y * terms[-1] + terms[-2]
    for term in terms[-3::-1]:
        total = total * y + term
    return total


def cos_sin(turns):
    r = turns - jnp.floor(turns + 0.5)
    y = r * r
    return horner(COS, y), r * horner(SIN, y)


def table_turns(steps, bins):
    return ((steps * bins) & (NT - 1)).astype(jnp.float32) * (1.0 / NT)


def spectrum_kernel(
    where_ref, signals_ref, bins_ref, gain_ref, damping_ref, damping_up_ref, stations_ref,
    send_ref, spec_ref, windowed, tables, hann, twiddle, later, group,
):
    sensors = spec_ref.shape[1]
    slices = send_ref.shape[0]
    q = pl.program_id(0)
    row = lax.broadcasted_iota(jnp.int32, (128, 128), 0)
    lane = lax.broadcasted_iota(jnp.int32, (128, 128), 1)

    @pl.when(q == 0)
    def _():
        times = (row * 128 + lane).astype(jnp.float32)
        hann[...] = 0.5 - 0.5 * cos_sin(times * (1.0 / NT))[0]
        for a in range(0, 128, 2):
            pair = [
                signals_ref[:, pl.ds(n * 128, 128)].astype(jnp.float32) * hann[n:n + 1, :]
                for n in (a, a + 1)
            ]
            windowed[pl.ds(a * sensors, 2 * sensors), :] = jnp.concatenate(
                pair, axis=0
            ).astype(jnp.bfloat16)
        groups = BLOCK // GROUP
        for g in range(groups):
            product = jnp.ones((1, damping_ref.shape[1]), jnp.float32)
            for k in range(g * GROUP + GROUP - 1, g * GROUP - 1, -1):
                later[k:k + 1, :] = product
                product = product * damping_ref[k:k + 1, :]
            group[g:g + 1, :] = product
            product = jnp.ones((1, damping_ref.shape[1]), jnp.float32)
            for k in range(g * GROUP, g * GROUP + GROUP):
                later[BLOCK + k:BLOCK + k + 1, :] = product
                product = product * damping_up_ref[k:k + 1, :]
            group[groups + g:groups + g + 1, :] = product
        stations = (stations_ref[...] - where_ref[1]).astype(jnp.float32)
        stations = jnp.concatenate([stations, stations + 64.0], axis=1)
        chosen = jnp.where(row.astype(jnp.float32) == stations, 1.0, 0.0).T
        gain = gain_ref[...].astype(jnp.float32)
        pick = functools.partial(
            jnp.dot, precision=lax.Precision.HIGHEST, preferred_element_type=jnp.float32
        )
        down = gain * pick(chosen[:64, :BLOCK], later[:BLOCK, :])
        up = gain * pick(chosen[64:, 64:64 + BLOCK], later[BLOCK:, :])
        values = jnp.concatenate([down, up], axis=0).T
        tables[:, :SLICE, :128] = values.reshape(slices, SLICE, 128)
        high = group[...].astype(jnp.bfloat16).astype(jnp.float32)
        rest = group[...] - high
        middle = rest.astype(jnp.bfloat16).astype(jnp.float32)
        fill = jnp.zeros((128 - 6 * groups, high.shape[1]), jnp.float32)
        terms = jnp.concatenate([high, middle, rest - middle, fill], axis=0).T
        tables[:, :SLICE, 128:] = terms.reshape(slices, SLICE, 128)
        tables[:, SLICE:, :] = jnp.zeros((slices, 64 - SLICE, 256), jnp.float32)
        for n in range(slices):
            tables[n, SLICE:SLICE + 8, :128] = jnp.broadcast_to(stations, (8, 128))

    bins = bins_ref[pl.ds(q, 1), :]
    c1, s1 = cos_sin(table_turns(row, bins))
    table = jnp.concatenate(
        [(c1 * (1 / 128)).astype(jnp.bfloat16), (s1 * (-1 / 128)).astype(jnp.bfloat16)], axis=1
    )
    twiddle[0], twiddle[1] = cos_sin(table_turns(row * 128, bins))
    sums = [[jnp.zeros((sensors, TILE), jnp.float32)] * 2 for _ in range(2)]
    few = 16
    for a in range(0, 128, few):
        part = jnp.dot(
            windowed[pl.ds(a * sensors, few * sensors), :], table, preferred_element_type=jnp.float32
        )
        for n in range(few):
            rows = slice(n * sensors, (n + 1) * sensors)
            re, im = part[rows, :TILE], part[rows, TILE:]
            c, s = twiddle[0, a + n:a + n + 1, :], twiddle[1, a + n:a + n + 1, :]
            turned = turn_back(c, s, re, im)
            sums[n % 2] = [x + y for x, y in zip(sums[n % 2], turned)]
    own = jnp.concatenate([x + y for x, y in zip(*sums)], axis=1)
    spec_ref[0] = own
    rows = pl.ds(pl.multiple_of(where_ref[0] * 8, 8), 8)
    for n in range(slices):
        send_ref[n, 0] = jnp.concatenate([own, tables[n, rows, :]], axis=0).astype(jnp.bfloat16)


def spectrum(where, signals, freq_bins, gain, damping, damping_up, stations, slices):
    sensors = signals.shape[0]
    tiles = freq_bins.shape[0] // TILE
    bins = freq_bins.reshape(tiles, TILE)
    stations = stations.reshape(1, -1)
    whole = lambda a: pl.BlockSpec(a.shape, lambda q: (0, 0))
    return pl.pallas_call(
        spectrum_kernel,
        grid=(tiles,),
        in_specs=[
            pl.BlockSpec(memory_space=pltpu.SMEM),
            whole(signals),
            whole(bins),
            whole(gain),
            whole(damping),
            whole(damping_up),
            whole(stations),
        ],
        out_specs=[
            pl.BlockSpec((slices, 1, 16, 2 * TILE), lambda q: (0, q, 0, 0)),
            pl.BlockSpec((1, sensors, 2 * TILE), lambda q: (q, 0, 0)),
        ],
        out_shape=[
            jax.ShapeDtypeStruct((slices, tiles, 16, 2 * TILE), jnp.bfloat16),
            jax.ShapeDtypeStruct((tiles, sensors, 2 * TILE), jnp.float32),
        ],
        scratch_shapes=[
            pltpu.VMEM((sensors * 128, 128), jnp.bfloat16),
            pltpu.VMEM((slices, 64, 2 * TILE), jnp.float32),
            pltpu.VMEM((128, 128), jnp.float32),
            pltpu.VMEM((2, 128, TILE), jnp.float32),
            pltpu.VMEM((2 * BLOCK, gain.shape[1]), jnp.float32),
            pltpu.VMEM((2 * BLOCK // GROUP, gain.shape[1]), jnp.float32),
        ],
        compiler_params=pltpu.CompilerParams(vmem_limit_bytes=56 * MIB),
        cost_estimate=pl.CostEstimate(flops=2 * 10**9, bytes_accessed=10**6, transcendentals=0),
        name="spectrum",
    )(where, signals, bins, gain, damping, damping_up, stations)


def inverse_kernel(bins_ref, after_ref, out_ref):
    del after_ref
    bins = bins_ref[:, 0:1]
    lane = lax.broadcasted_iota(jnp.int32, (TILE, 128), 1)
    c1, s1 = cos_sin(table_turns(lane, bins))
    c2, s2 = cos_sin(table_turns(lane * 128 + (NT - TOUT), bins))
    c2, s2 = c2 * (1 / 32), s2 * (1 / 32)
    for n in range(TOUT // 128):
        c, s = c2[:, n:n + 1], s2[:, n:n + 1]
        columns = pl.ds(n * 128, 128)
        out_ref[:TILE, columns] = (c1 * c - s1 * s).astype(jnp.bfloat16)
        out_ref[TILE:, columns] = (-s1 * c - c1 * s).astype(jnp.bfloat16)


def inverse_table(freq_bins, after):
    tiles = freq_bins.shape[0] // TILE
    bins = jnp.broadcast_to(freq_bins[:, None], (tiles * TILE, 128))
    return pl.pallas_call(
        inverse_kernel,
        grid=(tiles,),
        in_specs=[
            pl.BlockSpec((TILE, 128), lambda q: (q, 0)),
            pl.BlockSpec(memory_space=pl.ANY),
        ],
        out_specs=pl.BlockSpec((2 * TILE, TOUT), lambda q: (q, 0)),
        out_shape=jax.ShapeDtypeStruct((tiles * 2 * TILE, TOUT), jnp.bfloat16),
        compiler_params=pltpu.CompilerParams(vmem_limit_bytes=24 * MIB),
        cost_estimate=pl.CostEstimate(flops=4 * 10**9, bytes_accessed=5 * 10**6, transcendentals=0),
        name="inverse_table",
    )(bins, after)


def turn(c, s, re, im):
    return c * re - s * im, c * im + s * re


def turn_back(c, s, re, im):
    return c * re + s * im, c * im - s * re


def step(rate, turned, f_re, f_im):
    return rate * turned[0] + f_re, rate * turned[1] + f_im


def march_kernel(
    recv_ref, rot_ref, out_ref, done_ref, staged, sent, gains, places, specs, products
):
    done_ref[...] = jnp.zeros_like(done_ref)
    tiles = 8
    blocks = recv_ref.shape[0] // tiles
    groups = BLOCK // GROUP

    def unpack(block, unused):
        got = [recv_ref[block * tiles + p].astype(jnp.float32) for p in range(tiles)]
        both = jnp.concatenate([rows[8:, :128] for rows in got[:SLICE // 8]], axis=0)
        gains[block] = both
        places[block] = got[SLICE // 8][8:, :128]
        specs[block] = jnp.concatenate([rows[:8] for rows in got] * 2, axis=0).astype(jnp.bfloat16)
        terms = jnp.concatenate([rows[8:, 128:] for rows in got[:SLICE // 8]], axis=0)
        rates = terms[:, :2 * groups] + terms[:, 2 * groups:4 * groups]
        products[block, :, :2 * groups] = rates + terms[:, 4 * groups:6 * groups]
        return unused

    lax.fori_loop(0, blocks, unpack, 0, unroll=4)

    def forcing(block, direction, stations):
        gain, local = gains[block], places[block, 0:1]
        chosen = jnp.concatenate(
            [jnp.where(local == jnp.float32(k + 64 * direction), gain, 0.0) for k in stations], axis=0
        ).astype(jnp.bfloat16)
        return jnp.dot(chosen, specs[block], preferred_element_type=jnp.float32)

    down_of = [range(n * GROUP, n * GROUP + GROUP) for n in range(groups)]
    up_of = [range(BLOCK - 1 - n * GROUP, BLOCK - 1 - n * GROUP - GROUP, -1) for n in range(groups)]

    def across(turning, rate, near, far, state, forces):
        re, im = forces[:SLICE, :TILE], forces[:SLICE, TILE:]
        for i in range(1, GROUP):
            rows = slice(i * SLICE, (i + 1) * SLICE)
            re, im = turning(*near, re, im)
            re, im = re + forces[rows, :TILE], im + forces[rows, TILE:]
        return step(rate, turning(*far, *state), re, im)

    def body(b, carry):
        down, up = carry
        last = blocks - 1 - b
        near = rot_ref[0], rot_ref[1]
        far = rot_ref[2], rot_ref[3]
        down_rates, up_rates = products[b], products[last]
        for n in range(groups):
            here = b * groups + n
            staged[here, 0, :SLICE, :] = down[0].astype(jnp.bfloat16)
            staged[here, 0, SLICE:, :] = down[1].astype(jnp.bfloat16)
            m = groups - 1 - n
            here = last * groups + m
            staged[here, 1, :SLICE, :] = up[0].astype(jnp.bfloat16)
            staged[here, 1, SLICE:, :] = up[1].astype(jnp.bfloat16)
            down = across(
                turn_back, down_rates[:, n:n + 1], near, far, down, forcing(b, 0, down_of[n])
            )
            rate = up_rates[:, groups + m:groups + m + 1]
            up = across(turn, rate, near, far, up, forcing(last, 1, up_of[n]))
        for direction, block in ((0, b), (1, last)):
            part = pl.ds(block * groups, groups), direction
            pltpu.make_async_copy(staged.at[part], out_ref.at[part], sent).start()
        return down, up

    zero = jnp.zeros((SLICE, TILE), jnp.float32)
    lax.fori_loop(0, blocks, body, ((zero, zero), (zero, zero)))
    pltpu.make_async_copy(staged, out_ref, sent).wait()


def entering_states(recv, rot, blocks):
    shape = (blocks * BLOCK // GROUP, 2, 2 * SLICE, TILE)
    entering, done = pl.pallas_call(
        march_kernel,
        out_shape=[
            jax.ShapeDtypeStruct(shape, jnp.bfloat16),
            jax.ShapeDtypeStruct((8, 128), jnp.float32),
        ],
        in_specs=[pl.BlockSpec(memory_space=pltpu.VMEM)] * 2,
        out_specs=[pl.BlockSpec(memory_space=pl.ANY), pl.BlockSpec(memory_space=pltpu.VMEM)],
        scratch_shapes=[
            pltpu.VMEM(shape, jnp.bfloat16),
            pltpu.SemaphoreType.DMA,
            pltpu.VMEM((blocks, SLICE, 128), jnp.float32),
            pltpu.VMEM((blocks, 8, 128), jnp.float32),
            pltpu.VMEM((blocks, 128, 2 * TILE), jnp.bfloat16),
            pltpu.VMEM((blocks, SLICE, 128), jnp.float32),
        ],
        compiler_params=pltpu.CompilerParams(vmem_limit_bytes=56 * MIB),
        cost_estimate=pl.CostEstimate(flops=12 * 10**9, bytes_accessed=5 * 10**6, transcendentals=0),
        name="entering_states",
    )(recv, rot)
    return entering.reshape((-1,) + shape[2:]), done


TURN = GROUP + OWN
SKIP = TURN + 1


def local_kernel(
    gain_ref, rates_ref, spec_ref, omega_ref, after_ref, part_ref, rot_ref, done_ref, force, kept
):
    del after_ref
    done_ref[...] = jnp.zeros_like(done_ref)
    pair = force.shape[0]
    rates = rates_ref[0]

    def two(n, unused):
        for p in range(pair):
            q = n * pair + p
            force[p] = jnp.dot(gain_ref[0], spec_ref[q], preferred_element_type=jnp.float32)
        for p in range(pair):
            q = n * pair + p

            def forced(i):
                rows = pl.ds(i * SLICE, SLICE)
                return force[p, rows, :TILE], force[p, rows, TILE:]

            c, s = cos_sin(omega_ref[q, 0:1, :] * rates[:, TURN:TURN + 1])
            rot_ref[0, q, :SLICE, :] = c
            rot_ref[0, q, SLICE:, :] = s
            re, im = forced(GROUP - 1)
            kept[p, 0, 0], kept[p, 0, 1] = re, im
            for i in range(1, OWN):
                re, im = step(
                    rates[:, GROUP + i:GROUP + i + 1], turn_back(c, s, re, im),
                    *forced(GROUP - 1 - i),
                )
                kept[p, i, 0], kept[p, i, 1] = re, im
            re, im = forced(0)
            for i in range(1, GROUP):
                re, im = step(rates[:, i:i + 1], turn(c, s, re, im), *forced(i))
                if i >= GROUP - OWN:
                    n_own, n_near = i - (GROUP - OWN), GROUP - 1 - i
                    part_ref[0, q, n_own, :SLICE, :] = (re + kept[p, n_near, 0]).astype(jnp.bfloat16)
                    part_ref[0, q, n_own, SLICE:, :] = (im + kept[p, n_near, 1]).astype(jnp.bfloat16)
        return unused

    lax.fori_loop(0, spec_ref.shape[0] // pair, two, 0)


def local_states(gain, rates, spec, omega, after):
    slices, tiles = gain.shape[0], spec.shape[0]
    whole = lambda a: pl.BlockSpec(a.shape, lambda t: (0,) * a.ndim)
    return pl.pallas_call(
        local_kernel,
        grid=(slices,),
        in_specs=[
            pl.BlockSpec((1, GROUP * SLICE, 64), lambda t: (t, 0, 0)),
            pl.BlockSpec((1, SLICE, 128), lambda t: (t, 0, 0)),
            whole(spec),
            whole(omega),
            pl.BlockSpec(memory_space=pl.ANY),
        ],
        out_specs=[
            pl.BlockSpec((1, tiles, OWN, 2 * SLICE, TILE), lambda t: (t, 0, 0, 0, 0)),
            pl.BlockSpec((1, tiles, 2 * SLICE, TILE), lambda t: (t, 0, 0, 0)),
            pl.BlockSpec((8, 128), lambda t: (0, 0)),
        ],
        out_shape=[
            jax.ShapeDtypeStruct((slices, tiles, OWN, 2 * SLICE, TILE), jnp.bfloat16),
            jax.ShapeDtypeStruct((slices, tiles, 2 * SLICE, TILE), jnp.float32),
            jax.ShapeDtypeStruct((8, 128), jnp.float32),
        ],
        scratch_shapes=[
            pltpu.VMEM((2, GROUP * SLICE, 2 * TILE), jnp.float32),
            pltpu.VMEM((2, OWN, 2, SLICE, TILE), jnp.float32),
        ],
        compiler_params=pltpu.CompilerParams(vmem_limit_bytes=52 * MIB),
        cost_estimate=pl.CostEstimate(flops=20 * 10**9, bytes_accessed=20 * 10**6, transcendentals=0),
        name="local_states",
    )(gain, rates, spec, omega, after)


def estimate_kernel(
    core_ref, near_ref, far_ref, part_ref, rot_ref, rates_ref, inverse_ref, out_ref,
    even, odd, kept, inverse, ready,
):
    per, tiles = near_ref.shape[:2]
    height = per * SLICE
    index, last = pl.program_id(0), pl.num_programs(0) - 1
    core = core_ref[0]
    pieces = TOUT // 256

    def fill(state, q):
        lane = q * 2 * TILE
        for t in range(per):
            rates = rates_ref[t]
            c, s = rot_ref[t, q, :SLICE, :], rot_ref[t, q, SLICE:, :]
            re = near_ref[t, q, :SLICE, :].astype(jnp.float32)
            im = near_ref[t, q, SLICE:, :].astype(jnp.float32)
            for i in range(OWN):
                rate = rates[:, GROUP + i:GROUP + i + 1]
                re, im = turn_back(c, s, re, im)
                re, im = rate * re, rate * im
                kept[t, i, 0], kept[t, i, 1] = re, im
            c4, s4 = turn(c, s, c, s)
            c4, s4 = turn(c4, s4, c4, s4)
            re = far_ref[t, q, :SLICE, :].astype(jnp.float32)
            im = far_ref[t, q, SLICE:, :].astype(jnp.float32)
            re, im = turn(c4, s4, re, im)
            skip = rates[:, SKIP:SKIP + 1]
            re, im = skip * re, skip * im
            for i in range(OWN):
                rate = rates[:, GROUP - OWN + i:GROUP - OWN + i + 1]
                re, im = turn(c, s, re, im)
                re, im = rate * re, rate * im
                n = OWN - 1 - i
                rows = pl.ds(i * height + t * SLICE, SLICE)
                whole_re = re + kept[t, n, 0] + part_ref[t, q, i, :SLICE, :].astype(jnp.float32)
                whole_im = im + kept[t, n, 1] + part_ref[t, q, i, SLICE:, :].astype(jnp.float32)
                state[rows, lane:lane + TILE] = whole_re.astype(jnp.bfloat16)
                state[rows, lane + TILE:lane + 2 * TILE] = whole_im.astype(jnp.bfloat16)

    def multiply(state, n):
        columns = slice(n * 256, (n + 1) * 256)
        out = jnp.dot(state[...], inverse[:, columns], preferred_element_type=jnp.float32)
        for i in range(OWN):
            own = jnp.where(core == 0, OWN - 1 - i, i)
            out_ref[own, :, columns] = out[i * height:(i + 1) * height].astype(jnp.bfloat16)

    def both(filled, multiplied):
        for n in range(pieces):
            if multiplied is not None:
                multiply(multiplied, n)
            if filled is not None:
                for p in range(tiles // pieces):
                    fill(filled, n * (tiles // pieces) + p)

    fetch = pltpu.make_async_copy(inverse_ref, inverse, ready)
    inner = (index > 0) & (index < last)

    @pl.when(index == 0)
    def _():
        fetch.start()
        both(even, None)
        fetch.wait()

    pl.when(inner & (index % 2 == 1))(lambda: both(odd, even))
    pl.when(inner & (index % 2 == 0))(lambda: both(even, odd))
    pl.when(index == last)(lambda: both(None, odd))


def estimates(core, near, far, part, rot, rates, inverse):
    slices, tiles = near.shape[:2]
    per = 2
    steps = slices // per
    assert steps % 2 == 0
    here = lambda i: jnp.minimum(i, steps - 1)
    return pl.pallas_call(
        estimate_kernel,
        grid=(steps + 1,),
        in_specs=[
            pl.BlockSpec(memory_space=pltpu.SMEM),
            pl.BlockSpec((per, tiles, 2 * SLICE, TILE), lambda i: (here(i), 0, 0, 0)),
            pl.BlockSpec((per, tiles, 2 * SLICE, TILE), lambda i: (here(i), 0, 0, 0)),
            pl.BlockSpec((per, tiles, OWN, 2 * SLICE, TILE), lambda i: (here(i), 0, 0, 0, 0)),
            pl.BlockSpec((per, tiles, 2 * SLICE, TILE), lambda i: (here(i), 0, 0, 0)),
            pl.BlockSpec((per, SLICE, 128), lambda i: (here(i), 0, 0)),
            pl.BlockSpec(memory_space=pl.ANY),
        ],
        out_specs=pl.BlockSpec((OWN, per * SLICE, TOUT), lambda i: (0, jnp.maximum(i - 1, 0), 0)),
        out_shape=jax.ShapeDtypeStruct((OWN, slices * SLICE, TOUT), jnp.bfloat16),
        scratch_shapes=[
            pltpu.VMEM((OWN * per * SLICE, 2 * tiles * TILE), jnp.bfloat16),
            pltpu.VMEM((OWN * per * SLICE, 2 * tiles * TILE), jnp.bfloat16),
            pltpu.VMEM((per, OWN, 2, SLICE, TILE), jnp.float32),
            pltpu.VMEM(inverse.shape, inverse.dtype),
            pltpu.SemaphoreType.DMA,
        ],
        compiler_params=pltpu.CompilerParams(vmem_limit_bytes=40 * MIB),
        cost_estimate=pl.CostEstimate(flops=20 * 10**9, bytes_accessed=40 * 10**6, transcendentals=0),
        name="estimates",
    )(core, near, far, part, rot, rates, inverse)


def on_device(signals, freq_bins, sensor_station, gain, damping, damping_up, phase_speed):
    st, z, core = (lax.axis_index(axis) for axis in ALL)
    blocks = lax.axis_size("st")
    tiles = freq_bins.shape[0] // TILE
    sensors = sensor_station.shape[0]

    fq = (z * 2 + core).astype(jnp.int32)
    where = jnp.stack([fq, (st * BLOCK).astype(jnp.int32)])
    send, spec = spectrum(
        where, signals, freq_bins, gain, damping, damping_up, sensor_station, blocks
    )
    send = send.reshape((blocks * tiles,) + send.shape[2:])
    recv = lax.all_to_all(send, ALL, split_axis=0, concat_axis=0, tiled=True)
    spec_block = lax.all_gather(spec.astype(jnp.bfloat16), FQ)
    spec_block = spec_block.transpose(1, 0, 2, 3).reshape(tiles, sensors, 2 * TILE)

    omega = (freq_bins.astype(jnp.float32) / NT).reshape(tiles, 1, TILE)
    own_omega = lax.dynamic_index_in_dim(omega, fq, 0, keepdims=False)
    own_speed = lax.dynamic_slice_in_dim(phase_speed, st * SLICE, SLICE)
    theta = 2 * math.pi * own_omega * own_speed[:, None]
    past = theta * GROUP
    rot = jnp.stack([jnp.cos(theta), jnp.sin(theta), jnp.cos(past), jnp.sin(past)])
    recv, spec_block = lax.optimization_barrier((recv, spec_block))

    entering, done = entering_states(recv, rot, blocks)
    near = lax.all_to_all(entering, ALL, split_axis=0, concat_axis=0, tiled=True)
    damping, damping_up, gain, sensor_station, done = lax.optimization_barrier(
        (damping, damping_up, gain, sensor_station, done)
    )

    first = z * GROUP
    down = lax.dynamic_slice_in_dim(damping, first, GROUP)
    up = lax.dynamic_slice_in_dim(damping_up, first, GROUP)[::-1]
    far_rates = jnp.where(core == 0, up, down)
    near_rates = jnp.where(core == 0, down, up)[:OWN]
    speed = jnp.where(core == 0, phase_speed, -phase_speed)[None]
    skip = jnp.prod(far_rates[:GROUP - OWN], axis=0, keepdims=True)
    rates = jnp.concatenate([far_rates, near_rates, speed, skip], axis=0)
    rates = jnp.pad(rates, ((0, 128 - rates.shape[0]), (0, 0))).T.reshape(blocks, SLICE, 128)
    eight = lax.iota(jnp.int32, GROUP)
    far_order = first + jnp.where(core == 0, GROUP - 1 - eight, eight)
    local = sensor_station - st * BLOCK
    at = (local[None, :] == far_order[:, None])[None, :, None, :]
    own_gain = jnp.where(at, gain.T.reshape(blocks, 1, SLICE, sensors), 0)
    own_gain = own_gain.reshape(blocks, GROUP * SLICE, sensors)
    part, turns, done = local_states(
        own_gain, rates, spec_block, jnp.broadcast_to(omega, (tiles, 8, TILE)), done
    )
    inverse = inverse_table(freq_bins, done)
    near, part, turns = lax.optimization_barrier((near, part, turns))
    far = lax.ppermute(near, "core", [(0, 1), (1, 0)])
    shape = (blocks, tiles, 2 * SLICE, TILE)
    return estimates(
        core.reshape(1).astype(jnp.int32), near.reshape(shape), far.reshape(shape), part, turns,
        rates, inverse,
    )


def solution(mesh):
    torus = Mesh(mesh.devices.reshape(mesh.shape["st"], 4, 2), ALL)
    placed = (P(ALL, None), P(), P("st"), P("st", None), P("st", None), P("st", None), P())
    return jax.shard_map(
        on_device, mesh=torus, in_specs=placed, out_specs=P(ALL, None, None), check_vma=False
    )
```

time: 151 us -> 139 us (0.921)
  blocking collectives: 0 us -> 19.7 us
  waiting for transfers between devices: 20.2 us -> 7.87 us
  Pallas kernels: 86.7 us -> 75.2 us
  local copies, waits for them, and re-layouts: 12 us -> 5.75 us
    all_gather x0 -> x1, blocking collectives: none -> 19.7 us  [on_device(): spec_block = lax.all_gather(spec.astype(jnp.bfloat16), FQ)]
    all_to_all x1, waiting for transfers between devices: 14.9 us -> 0.01 us  [on_device(): recv = lax.all_to_all(send, ALL, split_axis=0, concat_axis=0, tiled=True)]
    all_to_all x1, waiting for transfers between devices: 0.01 us -> 7.16 us  [on_device(): lax.all_to_all(entering, ALL, split_axis=0, concat_axis=0, tiled=True)]
    pallas_call x1, Pallas kernels: 29.8 us -> 25 us  [estimates(): pl.pallas_call(estimate_kernel, grid=(steps + 1,), in_specs=[pl.BlockSpec...]
    ppermute x1, waiting for transfers between devices: 5.29 us -> 0.71 us  [on_device(): far = lax.ppermute(near, 'core', [(0, 1), (1, 0)])]
    all_to_all x1 -> x0, starting transfers between devices: 4.5 us -> none  [on_device(): lax.all_to_all(to_fq, FQ, split_axis=0, concat_axis=0, tiled=True)]
    all_to_all x1, starting transfers between devices: 5.09 us -> 8.84 us  [on_device(): lax.all_to_all(entering, ALL, split_axis=0, concat_axis=0, tiled=True)]
    pallas_call x1, Pallas kernels: 17.4 us -> 13.9 us  [entering_states(): pl.pallas_call(march_kernel, out_shape=[jax.ShapeDtypeStruct(shape, jnp.b...]
  transfers between devices with their start and end apart: 4 -> 3, of which waited for: 2 -> 2; matrix products, arithmetic and copies ran while one was open for 9% -> 8% of each run, Pallas kernels for 34% -> 21%
where the time goes in v3:
time: 139 us; the launch traced here: 138 us
  Pallas kernels  75.2 us (54%)
  starting transfers between devices  21.6 us (16%)
  blocking collectives  19.7 us (14%)
  waiting for transfers between devices  7.87 us (6%)
  other arithmetic  7.59 us (5%)
  local copies, waits for them, and re-layouts  5.75 us (4%)
    pallas_call x1, Pallas kernels, local_states(): pl.pallas_call(local_kernel, grid=(slices,), in_specs=[pl.BlockSpec((1, G...  25.2 us
    pallas_call x1, Pallas kernels, estimates(): pl.pallas_call(estimate_kernel, grid=(steps + 1,), in_specs=[pl.BlockSpec...  25 us
    all_gather x1, blocking collectives, on_device(): spec_block = lax.all_gather(spec.astype(jnp.bfloat16), FQ)  19.7 us
    pallas_call x1, Pallas kernels, entering_states(): pl.pallas_call(march_kernel, out_shape=[jax.ShapeDtypeStruct(shape, jnp.b...  13.9 us
    all_to_all x1, starting transfers between devices, on_device(): recv = lax.all_to_all(send, ALL, split_axis=0, concat_axis=0, tiled=True)  11.5 us
    all_to_all x1, starting transfers between devices, on_device(): lax.all_to_all(entering, ALL, split_axis=0, concat_axis=0, tiled=True)  8.84 us
    all_to_all x1, waiting for transfers between devices, on_device(): lax.all_to_all(entering, ALL, split_axis=0, concat_axis=0, tiled=True)  7.16 us
    pallas_call x1, Pallas kernels, spectrum(): pl.pallas_call(spectrum_kernel, grid=(tiles,), in_specs=[pl.BlockSpec(mem...  6.83 us
  transfers between devices with their start and end apart: 3, of which 2 were waited for; matrix products, arithmetic and copies ran while one was open for 8% of the time, Pallas kernels for 21%

profile of v3, /device:TPU:1, one launch (start us, length us, event | category | flops | bytes accessed | tf_op | source)
XLA Modules:
  0.0 138.1 jit_solution(17365084914951525976)
XLA Ops:
  0.0 0.6 pad_add_fusion.where_ref
  0.6 0.0 copy-start.5
  0.6 0.0 copy-start.4
  0.6 6.8 %spectrum.1 = (bf16[16,8,16,256]{3,2,1,0:T(8,128)(2,1)}, f32[8,8,256]{2,1,0:T(8,128)}) custom-call(s32[2]{0:T(128)} %pad_add_fusion.where_ref, bf16[8,16384]{1,0:T(8,128)(2,1)} %signals_ref.1, s32[8,128]{1,0:T(8,128)} %bitcast.39, bf16[64,768]{1,0:T(8,128)(2,1)} %gain_ref.1, f32[32,768]{1,0:T(8,128)} %damping_ref.1, f32[32,768]{1,0:T(8,128)} %damping_up_ref.1, ...), custom_call_target="tpu_custom_call" | custom-call | flops 2000000000 | bytes 1000000 | tf_op jit(solution)/shard_map/spectrum/pallas_call | solution.py:132
  7.4 11.5 %all-to-all-start = ((bf16[128,16,256]{2,1,0:T(8,128)(2,1)}), bf16[128,16,256]{2,1,0:T(8,128)(2,1)S(1)}, u32[]{:S(2)}, u32[]{:S(2)}) async-start(bf16[128,16,256]{2,1,0:T(8,128)(2,1)} %bitcast.34), calls=%async_computation | async-start | bytes 2097152 | tf_op jit(solution)/shard_map/all_to_all | solution.py:496
  18.9 0.0 copy-done.5
  18.9 0.1 dynamic_slice.14
  19.0 0.8 convert_element_type.10
  19.9 19.7 %all-gather = bf16[64,8,256]{2,1,0:T(8,128)(2,1)S(1)} all-gather(bf16[8,8,256]{2,1,0:T(8,128)(2,1)S(1)} %convert_element_type.10), channel_id=2, replica_groups=mesh['st'=16,'z'=4,'core'=2] {'z','core'}, dimensions={0}, use_global_device_ids=true | all-gather | bytes 294912 | tf_op jit(solution)/shard_map/all_gather | solution.py:497
  39.6 0.7 copy.19
  40.3 0.0 copy-done.4
  40.3 0.3 multiply_cosine_fusion
  40.6 0.6 pad_maximum_fusion.rot_ref
  41.2 0.0 all-to-all-done.recv_ref
  41.2 0.0 copy-start.2
  41.2 1.0 copy-done.2
  42.2 13.9 %entering_states.1 = (bf16[64,2,96,128]{3,2,1,0:T(8,128)(2,1)}, f32[8,128]{1,0:T(8,128)}) custom-call(bf16[128,16,256]{2,1,0:T(8,128)(2,1)} %copy-done.2, f32[4,48,128]{2,1,0:T(8,128)} %pad_maximum_fusion.rot_ref), custom_call_target="tpu_custom_call" | custom-call | flops 12000000000 | bytes 5000000 | tf_op jit(solution)/shard_map/entering_states/pallas_call | solution.py:280
  56.1 0.0 copy-start.3
  56.1 8.8 %all-to-all-start.1 = ((bf16[128,96,128]{2,1,0:T(8,128)(2,1)}), bf16[128,96,128]{2,1,0:T(8,128)(2,1)S(1)}, u32[]{:S(2)}, u32[]{:S(2)}) async-start(bf16[128,96,128]{2,1,0:T(8,128)(2,1)} %bitcast.33), calls=%async_computation.1 | async-start | bytes 6291456 | tf_op jit(solution)/shard_map/all_to_all | solution.py:509
  64.9 0.0 copy-start.1
  65.0 0.7 constant_dynamic-slice_fusion
  65.7 0.1 rev.3
  65.8 0.7 dynamic-slice_select_fusion
  66.6 0.0 copy-done.3
  66.6 0.8 copy.17
  67.4 0.7 slice_select_fusion
  68.1 0.8 fusion
  68.9 1.1 copy.16
  70.1 0.7 broadcast_subtract_fusion
  70.7 0.1 broadcast_compare_fusion
  70.8 2.2 %bitcast_select_fusion.gain_ref = bf16[16,384,64]{2,1,0:T(8,128)(2,1)} fusion(pred[384,64]{1,0:T(8,128)(4,1)S(1)} %bitcast.37, bf16[16,48,64]{2,1,0:T(8,128)(2,1)} %bitcast.36), kind=kLoop, calls=%fused_computation | loop fusion | flops 393216 | bytes 909312 | tf_op jit(solution)/shard_map/jit(_where)/select_n | solution.py:527
  73.0 0.0 copy-done.1
  73.0 0.0 copy-start
  73.0 0.9 copy-done
  74.0 25.2 %local_states.1 = (bf16[16,8,4,96,128]{4,3,2,1,0:T(8,128)(2,1)}, f32[16,8,96,128]{3,2,1,0:T(8,128)}, f32[8,128]{1,0:T(8,128)S(1)}) custom-call(bf16[16,384,64]{2,1,0:T(8,128)(2,1)} %bitcast_select_fusion.gain_ref, f32[16,48,128]{2,1,0:T(8,128)S(1)} %bitcast.29, bf16[8,64,256]{2,1,0:T(8,128)(2,1)S(1)} %bitcast.31, ...), custom_call_target="tpu_custom_call" | custom-call | flops 20000000000 | bytes 20000000 | tf_op jit(solution)/shard_map/local_states/pallas_call | solution.py:352
  99.2 7.2 %all-to-all-done.1 = bf16[128,96,128]{2,1,0:T(8,128)(2,1)S(1)} async-done(((bf16[128,96,128]{2,1,0:T(8,128)(2,1)}), bf16[128,96,128]{2,1,0:T(8,128)(2,1)S(1)}, u32[]{:S(2)}, u32[]{:S(2)}) %all-to-all-start.1) | async-done | bytes 3145760 | tf_op jit(solution)/shard_map/all_to_all | solution.py:509
  106.4 1.3 collective-permute-start
  107.7 0.2 broadcast_in_dim.62.bins_ref
  107.9 4.4 %inverse_table.1.inverse_ref = bf16[2048,1024]{1,0:T(8,128)(2,1)S(1)} custom-call(s32[1024,128]{1,0:T(8,128)S(1)} %broadcast_in_dim.62.bins_ref, f32[8,128]{1,0:T(8,128)S(1)} %get-tuple-element.38.after_ref), custom_call_target="tpu_custom_call" | custom-call | flops 4000000000 | bytes 5000000 | tf_op jit(solution)/shard_map/inverse_table/pallas_call | solution.py:183
  112.3 0.7 collective-permute-done
  113.0 25.0 %estimates.1 = bf16[4,768,1024]{2,1,0:T(8,128)(2,1)} custom-call(s32[1]{0:T(128)} %bitcast.core_ref, bf16[16,8,96,128]{3,2,1,0:T(8,128)(2,1)S(1)} %bitcast.28, bf16[16,8,96,128]{3,2,1,0:T(8,128)(2,1)S(1)} %bitcast.32, bf16[16,8,4,96,128]{4,3,2,1,0:T(8,128)(2,1)} %get-tuple-element.36.part_ref, f32[16,8,96,128]{3,2,1,0:T(8,128)} %get-tuple-element.37.rot_ref, ...), custom_call_target="tpu_custom_call" | custom-call | flops 20000000000 | bytes 40000000 | tf_op jit(solution)/shard_map/estimates/pallas_call | solution.py:457
  (9 shorter events, 0.1 us)
Async XLA Ops:
  0.6 18.3 %copy-start.5 = (f32[768]{0:T(1024)S(1)}, f32[768]{0:T(1024)}, u32[]{:S(2)}) copy-start(f32[768]{0:T(1024)} %param.13) | copy-start | bytes 9220
  0.6 39.7 %copy-start.4 = (s32[1024]{0:T(1024)S(1)}, s32[1024]{0:T(1024)}, u32[]{:S(2)}) copy-start(s32[1024]{0:T(1024)} %param.8) | copy-start | bytes 12292
  7.4 33.8 %all-to-all-start = ((bf16[128,16,256]{2,1,0:T(8,128)(2,1)}), bf16[128,16,256]{2,1,0:T(8,128)(2,1)S(1)}, u32[]{:S(2)}, u32[]{:S(2)}) async-start(bf16[128,16,256]{2,1,0:T(8,128)(2,1)} %bitcast.34), calls=%async_computation | async-start | bytes 2097152 | tf_op jit(solution)/shard_map/all_to_all | solution.py:496
  41.2 1.0 copy-start.2
  56.1 10.5 %copy-start.3 = (bf16[64,768]{1,0:T(8,128)(2,1)S(1)}, bf16[64,768]{1,0:T(8,128)(2,1)}, u32[]{:S(2)}) copy-start(bf16[64,768]{1,0:T(8,128)(2,1)} %gain_ref.1) | copy-start | bytes 294916
  56.1 50.3 %all-to-all-start.1 = ((bf16[128,96,128]{2,1,0:T(8,128)(2,1)}), bf16[128,96,128]{2,1,0:T(8,128)(2,1)S(1)}, u32[]{:S(2)}, u32[]{:S(2)}) async-start(bf16[128,96,128]{2,1,0:T(8,128)(2,1)} %bitcast.33), calls=%async_computation.1 | async-start | bytes 6291456 | tf_op jit(solution)/shard_map/all_to_all | solution.py:509
  64.9 8.1 %copy-start.1 = (f32[8,128]{1,0:T(8,128)S(1)}, f32[8,128]{1,0:T(8,128)}, u32[]{:S(2)}) copy-start(f32[8,128]{1,0:T(8,128)} %get-tuple-element.32.after_ref) | copy-start | bytes 12292
  73.0 1.0 copy-start
  106.4 6.6 %collective-permute-start = (bf16[128,96,128]{2,1,0:T(8,128)(2,1)S(1)}, bf16[128,96,128]{2,1,0:T(8,128)(2,1)S(1)}, u32[]{:S(2)}, u32[]{:S(2)}) collective-permute-start(bf16[128,96,128]{2,1,0:T(8,128)(2,1)S(1)} %all-to-all-done.1), channel_id=1, source_target_pairs={{0,1},{1,0},{2,3},{3,2},{4,5},{5,4},{6,7},{7,6},{8,9},{9,8},{10,11... | collective-permute-start | bytes 9437192 | tf_op jit(solution)/shard_map/ppermute | solution.py:534

commit v4 on v3

--- a/solution.py
+++ b/solution.py
@@ -47,7 +47,7 @@
     where_ref, signals_ref, bins_ref, gain_ref, damping_ref, damping_up_ref, stations_ref,
     send_ref, spec_ref, windowed, tables, hann, twiddle, later, group,
 ):
-    sensors = spec_ref.shape[1]
+    sensors = signals_ref.shape[0]
     slices = send_ref.shape[0]
     q = pl.program_id(0)
     row = lax.broadcasted_iota(jnp.int32, (128, 128), 0)
@@ -98,40 +98,44 @@
         for n in range(slices):
             tables[n, SLICE:SLICE + 8, :128] = jnp.broadcast_to(stations, (8, 128))
 
-    bins = bins_ref[pl.ds(q, 1), :]
-    c1, s1 = cos_sin(table_turns(row, bins))
-    table = jnp.concatenate(
-        [(c1 * (1 / 128)).astype(jnp.bfloat16), (s1 * (-1 / 128)).astype(jnp.bfloat16)], axis=1
-    )
-    twiddle[0], twiddle[1] = cos_sin(table_turns(row * 128, bins))
-    sums = [[jnp.zeros((sensors, TILE), jnp.float32)] * 2 for _ in range(2)]
-    few = 16
-    for a in range(0, 128, few):
-        part = jnp.dot(
-            windowed[pl.ds(a * sensors, few * sensors), :], table, preferred_element_type=jnp.float32
+    each = spec_ref.shape[0]
+    for p in range(each):
+        bins = bins_ref[pl.ds(q * each + p, 1), :]
+        c1, s1 = cos_sin(table_turns(row, bins))
+        table = jnp.concatenate(
+            [(c1 * (1 / 128)).astype(jnp.bfloat16), (s1 * (-1 / 128)).astype(jnp.bfloat16)], axis=1
         )
-        for n in range(few):
-            rows = slice(n * sensors, (n + 1) * sensors)
-            re, im = part[rows, :TILE], part[rows, TILE:]
-            c, s = twiddle[0, a + n:a + n + 1, :], twiddle[1, a + n:a + n + 1, :]
-            turned = turn_back(c, s, re, im)
-            sums[n % 2] = [x + y for x, y in zip(sums[n % 2], turned)]
-    own = jnp.concatenate([x + y for x, y in zip(*sums)], axis=1)
-    spec_ref[0] = own
-    rows = pl.ds(pl.multiple_of(where_ref[0] * 8, 8), 8)
-    for n in range(slices):
-        send_ref[n, 0] = jnp.concatenate([own, tables[n, rows, :]], axis=0).astype(jnp.bfloat16)
+        twiddle[p, 0], twiddle[p, 1] = cos_sin(table_turns(row * 128, bins))
+        sums = [[jnp.zeros((sensors, TILE), jnp.float32)] * 2 for _ in range(2)]
+        few = 16
+        for a in range(0, 128, few):
+            part = jnp.dot(
+                windowed[pl.ds(a * sensors, few * sensors), :], table, preferred_element_type=jnp.float32
+            )
+            for n in range(few):
+                rows = slice(n * sensors, (n + 1) * sensors)
+                re, im = part[rows, :TILE], part[rows, TILE:]
+                c, s = twiddle[p, 0, a + n:a + n + 1, :], twiddle[p, 1, a + n:a + n + 1, :]
+                turned = turn_back(c, s, re, im)
+                sums[n % 2] = [x + y for x, y in zip(sums[n % 2], turned)]
+        both = [x + y for x, y in zip(*sums)]
+        spec_ref[p] = jnp.concatenate(both, axis=0).astype(jnp.bfloat16)
+        own = jnp.concatenate(both, axis=1)
+        rows = pl.ds(pl.multiple_of(where_ref[0] * 8, 8), 8)
+        for n in range(slices):
+            send_ref[n, p] = jnp.concatenate([own, tables[n, rows, :]], axis=0).astype(jnp.bfloat16)
 
 
 def spectrum(where, signals, freq_bins, gain, damping, damping_up, stations, slices):
     sensors = signals.shape[0]
     tiles = freq_bins.shape[0] // TILE
+    each = 2
     bins = freq_bins.reshape(tiles, TILE)
     stations = stations.reshape(1, -1)
     whole = lambda a: pl.BlockSpec(a.shape, lambda q: (0, 0))
     return pl.pallas_call(
         spectrum_kernel,
-        grid=(tiles,),
+        grid=(tiles // each,),
         in_specs=[
             pl.BlockSpec(memory_space=pltpu.SMEM),
             whole(signals),
@@ -142,18 +146,18 @@
             whole(stations),
         ],
         out_specs=[
-            pl.BlockSpec((slices, 1, 16, 2 * TILE), lambda q: (0, q, 0, 0)),
-            pl.BlockSpec((1, sensors, 2 * TILE), lambda q: (q, 0, 0)),
+            pl.BlockSpec((slices, each, 16, 2 * TILE), lambda q: (0, q, 0, 0)),
+            pl.BlockSpec((each, 2 * sensors, TILE), lambda q: (q, 0, 0)),
         ],
         out_shape=[
             jax.ShapeDtypeStruct((slices, tiles, 16, 2 * TILE), jnp.bfloat16),
-            jax.ShapeDtypeStruct((tiles, sensors, 2 * TILE), jnp.float32),
+            jax.ShapeDtypeStruct((tiles, 2 * sensors, TILE), jnp.bfloat16),
         ],
         scratch_shapes=[
             pltpu.VMEM((sensors * 128, 128), jnp.bfloat16),
             pltpu.VMEM((slices, 64, 2 * TILE), jnp.float32),
             pltpu.VMEM((128, 128), jnp.float32),
-            pltpu.VMEM((2, 128, TILE), jnp.float32),
+            pltpu.VMEM((each, 2, 128, TILE), jnp.float32),
             pltpu.VMEM((2 * BLOCK, gain.shape[1]), jnp.float32),
             pltpu.VMEM((2 * BLOCK // GROUP, gain.shape[1]), jnp.float32),
         ],
@@ -494,8 +498,9 @@
     )
     send = send.reshape((blocks * tiles,) + send.shape[2:])
     recv = lax.all_to_all(send, ALL, split_axis=0, concat_axis=0, tiled=True)
-    spec_block = lax.all_gather(spec.astype(jnp.bfloat16), FQ)
-    spec_block = spec_block.transpose(1, 0, 2, 3).reshape(tiles, sensors, 2 * TILE)
+    recv, spec_block = lax.optimization_barrier((recv, lax.all_gather(spec, FQ)))
+    spec_block = spec_block.reshape(tiles, tiles, 2, sensors // tiles, TILE)
+    spec_block = spec_block.transpose(1, 0, 3, 2, 4).reshape(tiles, sensors, 2 * TILE)
 
     omega = (freq_bins.astype(jnp.float32) / NT).reshape(tiles, 1, TILE)
     own_omega = lax.dynamic_index_in_dim(omega, fq, 0, keepdims=False)
@@ -503,8 +508,6 @@
     theta = 2 * math.pi * own_omega * own_speed[:, None]
     past = theta * GROUP
     rot = jnp.stack([jnp.cos(theta), jnp.sin(theta), jnp.cos(past), jnp.sin(past)])
-    recv, spec_block = lax.optimization_barrier((recv, spec_block))
-
     entering, done = entering_states(recv, rot, blocks)
     near = lax.all_to_all(entering, ALL, split_axis=0, concat_axis=0, tiled=True)
     damping, damping_up, gain, sensor_station, done = lax.optimization_barrier(

time: 139 us -> 136 us (0.978)
  transfers between devices with their start and end apart: 3 -> 3, of which waited for: 2 -> 2; matrix products, arithmetic and copies ran while one was open for 8% -> 7% of each run, Pallas kernels for 21% -> 22%
where the time goes in v4:
time: 136 us
  Pallas kernels  74.3 us (55%)
  starting transfers between devices  21.3 us (16%)
  blocking collectives  20 us (15%)
  waiting for transfers between devices  7.88 us (6%)
  other arithmetic  6.77 us (5%)
  local copies, waits for them, and re-layouts  5.12 us (4%)
    pallas_call x1, Pallas kernels, local_states(): pl.pallas_call(local_kernel, grid=(slices,), in_specs=[pl.BlockSpec((1, G...  25.2 us
    pallas_call x1, Pallas kernels, estimates(): pl.pallas_call(estimate_kernel, grid=(steps + 1,), in_specs=[pl.BlockSpec...  25 us
    all_gather x1, blocking collectives, on_device(): lax.all_gather(spec, FQ)  20 us
    pallas_call x1, Pallas kernels, entering_states(): pl.pallas_call(march_kernel, out_shape=[jax.ShapeDtypeStruct(shape, jnp.b...  13.9 us
    all_to_all x1, starting transfers between devices, on_device(): recv = lax.all_to_all(send, ALL, split_axis=0, concat_axis=0, tiled=True)  11.5 us
    all_to_all x1, starting transfers between devices, on_device(): lax.all_to_all(entering, ALL, split_axis=0, concat_axis=0, tiled=True)  8.45 us
    all_to_all x1, waiting for transfers between devices, on_device(): lax.all_to_all(entering, ALL, split_axis=0, concat_axis=0, tiled=True)  7.16 us
    pallas_call x1, Pallas kernels, spectrum(): pl.pallas_call(spectrum_kernel, grid=(tiles // each,), in_specs=[pl.Block...  5.88 us
  transfers between devices with their start and end apart: 3, of which 2 were waited for; matrix products, arithmetic and copies ran while one was open for 7% of the time, Pallas kernels for 22%

profile of v4, /device:TPU:1, one launch (start us, length us, event | category | flops | bytes accessed | tf_op | source)
XLA Modules:
  0.0 135.6 jit_solution(10443820895396724938)
XLA Ops:
  0.0 0.6 pad_add_fusion.where_ref
  0.6 0.0 copy-start.5
  0.6 0.0 copy-start.4
  0.6 5.9 %spectrum.1 = (bf16[16,8,16,256]{3,2,1,0:T(8,128)(2,1)}, bf16[8,16,128]{2,1,0:T(8,128)(2,1)}) custom-call(s32[2]{0:T(128)} %pad_add_fusion.where_ref, bf16[8,16384]{1,0:T(8,128)(2,1)} %signals_ref.1, s32[8,128]{1,0:T(8,128)} %bitcast.41, bf16[64,768]{1,0:T(8,128)(2,1)} %gain_ref.1, f32[32,768]{1,0:T(8,128)} %damping_ref.1, f32[32,768]{1,0:T(8,128)} %damping_up_ref.1, ...), custom_call_target="tpu_custom_call" | custom-call | flops 2000000000 | bytes 1000000 | tf_op jit(solution)/shard_map/spectrum/pallas_call | solution.py:136
  6.5 11.5 %all-to-all-start = ((bf16[128,16,256]{2,1,0:T(8,128)(2,1)}), bf16[128,16,256]{2,1,0:T(8,128)(2,1)S(1)}, u32[]{:S(2)}, u32[]{:S(2)}) async-start(bf16[128,16,256]{2,1,0:T(8,128)(2,1)} %bitcast.36), calls=%async_computation | async-start | bytes 2097152 | tf_op jit(solution)/shard_map/all_to_all | solution.py:500
  18.0 0.0 copy-done.5
  18.0 0.1 dynamic_slice.14
  18.1 0.0 copy-done.4
  18.2 0.3 multiply_cosine_fusion
  18.4 0.6 pad_maximum_fusion.rot_ref
  19.1 20.0 %all-gather = bf16[64,16,128]{2,1,0:T(8,128)(2,1)S(1)} all-gather(bf16[8,16,128]{2,1,0:T(8,128)(2,1)} %get-tuple-element.23), channel_id=2, replica_groups=mesh['st'=16,'z'=4,'core'=2] {'z','core'}, dimensions={0}, use_global_device_ids=true | all-gather | bytes 294912 | tf_op jit(solution)/shard_map/all_gather | solution.py:501
  39.1 0.0 all-to-all-done.recv_ref
  39.1 0.0 copy-start.2
  39.1 0.8 copy.19
  39.8 0.3 copy-done.2
  40.2 13.9 %entering_states.1 = (bf16[64,2,96,128]{3,2,1,0:T(8,128)(2,1)}, f32[8,128]{1,0:T(8,128)}) custom-call(bf16[128,16,256]{2,1,0:T(8,128)(2,1)} %copy-done.2, f32[4,48,128]{2,1,0:T(8,128)} %pad_maximum_fusion.rot_ref), custom_call_target="tpu_custom_call" | custom-call | flops 12000000000 | bytes 5000000 | tf_op jit(solution)/shard_map/entering_states/pallas_call | solution.py:284
  54.0 0.0 copy-start.3
  54.0 8.5 %all-to-all-start.1 = ((bf16[128,96,128]{2,1,0:T(8,128)(2,1)}), bf16[128,96,128]{2,1,0:T(8,128)(2,1)S(1)}, u32[]{:S(2)}, u32[]{:S(2)}) async-start(bf16[128,96,128]{2,1,0:T(8,128)(2,1)} %bitcast.35), calls=%async_computation.1 | async-start | bytes 6291456 | tf_op jit(solution)/shard_map/all_to_all | solution.py:512
  62.5 0.0 copy-start.1
  62.5 0.7 constant_dynamic-slice_fusion
  63.2 0.1 rev.3
  63.3 0.7 dynamic-slice_select_fusion
  64.1 0.0 copy-done.3
  64.1 0.8 copy.17
  64.9 0.7 slice_select_fusion
  65.7 0.8 fusion
  66.4 1.1 copy.15
  67.6 0.7 broadcast_subtract_fusion
  68.3 0.1 broadcast_compare_fusion
  68.4 2.2 %bitcast_select_fusion.gain_ref = bf16[16,384,64]{2,1,0:T(8,128)(2,1)} fusion(pred[384,64]{1,0:T(8,128)(4,1)S(1)} %bitcast.39, bf16[16,48,64]{2,1,0:T(8,128)(2,1)} %bitcast.38), kind=kLoop, calls=%fused_computation | loop fusion | flops 393216 | bytes 909312 | tf_op jit(solution)/shard_map/jit(_where)/select_n | solution.py:530
  70.6 0.0 copy-done.1
  70.6 0.0 copy-start
  70.6 0.9 copy-done
  71.5 25.2 %local_states.1 = (bf16[16,8,4,96,128]{4,3,2,1,0:T(8,128)(2,1)}, f32[16,8,96,128]{3,2,1,0:T(8,128)}, f32[8,128]{1,0:T(8,128)S(1)}) custom-call(bf16[16,384,64]{2,1,0:T(8,128)(2,1)} %bitcast_select_fusion.gain_ref, f32[16,48,128]{2,1,0:T(8,128)S(1)} %bitcast.31, bf16[8,64,256]{2,1,0:T(8,128)(2,1)S(1)} %bitcast.33, ...), custom_call_target="tpu_custom_call" | custom-call | flops 20000000000 | bytes 20000000 | tf_op jit(solution)/shard_map/local_states/pallas_call | solution.py:356
  96.7 7.2 %all-to-all-done.1 = bf16[128,96,128]{2,1,0:T(8,128)(2,1)S(1)} async-done(((bf16[128,96,128]{2,1,0:T(8,128)(2,1)}), bf16[128,96,128]{2,1,0:T(8,128)(2,1)S(1)}, u32[]{:S(2)}, u32[]{:S(2)}) %all-to-all-start.1) | async-done | bytes 3145760 | tf_op jit(solution)/shard_map/all_to_all | solution.py:512
  103.9 1.3 collective-permute-start
  105.2 0.2 broadcast_in_dim.62.bins_ref
  105.4 4.4 %inverse_table.1.inverse_ref = bf16[2048,1024]{1,0:T(8,128)(2,1)S(1)} custom-call(s32[1024,128]{1,0:T(8,128)S(1)} %broadcast_in_dim.62.bins_ref, f32[8,128]{1,0:T(8,128)S(1)} %get-tuple-element.38.after_ref), custom_call_target="tpu_custom_call" | custom-call | flops 4000000000 | bytes 5000000 | tf_op jit(solution)/shard_map/inverse_table/pallas_call | solution.py:187
  109.8 0.7 collective-permute-done
  110.5 25.0 %estimates.1 = bf16[4,768,1024]{2,1,0:T(8,128)(2,1)} custom-call(s32[1]{0:T(128)} %bitcast.core_ref, bf16[16,8,96,128]{3,2,1,0:T(8,128)(2,1)S(1)} %bitcast.30, bf16[16,8,96,128]{3,2,1,0:T(8,128)(2,1)S(1)} %bitcast.34, bf16[16,8,4,96,128]{4,3,2,1,0:T(8,128)(2,1)} %get-tuple-element.36.part_ref, f32[16,8,96,128]{3,2,1,0:T(8,128)} %get-tuple-element.37.rot_ref, ...), custom_call_target="tpu_custom_call" | custom-call | flops 20000000000 | bytes 40000000 | tf_op jit(solution)/shard_map/estimates/pallas_call | solution.py:461
  (9 shorter events, 0.1 us)
Async XLA Ops:
  0.6 17.4 %copy-start.5 = (f32[768]{0:T(1024)S(1)}, f32[768]{0:T(1024)}, u32[]{:S(2)}) copy-start(f32[768]{0:T(1024)} %param.13) | copy-start | bytes 9220
  0.6 17.5 %copy-start.4 = (s32[1024]{0:T(1024)S(1)}, s32[1024]{0:T(1024)}, u32[]{:S(2)}) copy-start(s32[1024]{0:T(1024)} %param.8) | copy-start | bytes 12292
  6.5 32.6 %all-to-all-start = ((bf16[128,16,256]{2,1,0:T(8,128)(2,1)}), bf16[128,16,256]{2,1,0:T(8,128)(2,1)S(1)}, u32[]{:S(2)}, u32[]{:S(2)}) async-start(bf16[128,16,256]{2,1,0:T(8,128)(2,1)} %bitcast.36), calls=%async_computation | async-start | bytes 2097152 | tf_op jit(solution)/shard_map/all_to_all | solution.py:500
  39.1 1.1 copy-start.2
  54.0 10.1 %copy-start.3 = (bf16[64,768]{1,0:T(8,128)(2,1)S(1)}, bf16[64,768]{1,0:T(8,128)(2,1)}, u32[]{:S(2)}) copy-start(bf16[64,768]{1,0:T(8,128)(2,1)} %gain_ref.1) | copy-start | bytes 294916
  54.0 49.9 %all-to-all-start.1 = ((bf16[128,96,128]{2,1,0:T(8,128)(2,1)}), bf16[128,96,128]{2,1,0:T(8,128)(2,1)S(1)}, u32[]{:S(2)}, u32[]{:S(2)}) async-start(bf16[128,96,128]{2,1,0:T(8,128)(2,1)} %bitcast.35), calls=%async_computation.1 | async-start | bytes 6291456 | tf_op jit(solution)/shard_map/all_to_all | solution.py:512
  62.5 8.1 %copy-start.1 = (f32[8,128]{1,0:T(8,128)S(1)}, f32[8,128]{1,0:T(8,128)}, u32[]{:S(2)}) copy-start(f32[8,128]{1,0:T(8,128)} %get-tuple-element.32.after_ref) | copy-start | bytes 12292
  70.6 1.0 copy-start
  103.9 6.6 %collective-permute-start = (bf16[128,96,128]{2,1,0:T(8,128)(2,1)S(1)}, bf16[128,96,128]{2,1,0:T(8,128)(2,1)S(1)}, u32[]{:S(2)}, u32[]{:S(2)}) collective-permute-start(bf16[128,96,128]{2,1,0:T(8,128)(2,1)S(1)} %all-to-all-done.1), channel_id=1, source_target_pairs={{0,1},{1,0},{2,3},{3,2},{4,5},{5,4},{6,7},{7,6},{8,9},{9,8},{10,11... | collective-permute-start | bytes 9437192 | tf_op jit(solution)/shard_map/ppermute | solution.py:537
